TPU v7x, 32 devices: a whole 2x2x4 slice. The times are simulated.
32 devices in a mesh: wide: 8 (over z, x), narrow: 4 (over y, core).
Axes of the slice: x: 2, y: 2, z: 4, core: 2. Of those that a mesh axis runs over, the one named last changes fastest.
Arguments:
- hidden_in: bfloat16 [12288, 768], P(('wide', 'narrow')), may hold values from -6 to 6
- seq_lengths: int32 [96], P(('wide', 'narrow')), may hold values from 64 to 128
- mask_positions: int32 [96, 38], P(('wide', 'narrow')), may hold values from 0 to 127, as said below
- mask_vector: bfloat16 [768], P('wide'), may hold values from -5 to 5
- cotangent: bfloat16 [12288, 768], P(('wide', 'narrow')), may hold values from -6 to 6
- norm_gain: bfloat16 [2, 2, 768], P(None, None, 'wide'), may hold values from 0.099609375 to 1.8984375
- norm_bias: bfloat16 [2, 2, 768], P(None, None, 'wide'), may hold values from -1.5 to 1.5
- in_right: bfloat16 [2, 2, 768, 192], P(None, None, 'wide'), may hold values from -0.4375 to 0.4375
- in_left: bfloat16 [2, 2, 768, 192], P(None, None, 'wide'), may hold values from -0.4375 to 0.4375
- conv_taps: bfloat16 [2, 3, 768], P(None, None, 'wide'), may hold values from -3.5 to 3.5
- skip_bias: bfloat16 [2, 768], P(None, 'wide'), may hold values from -4 to 4
- filter_in: bfloat16 [2, 5, 128], P(None, None, 'wide'), may hold values from -6 to 6
- filter_in_bias: bfloat16 [2, 128], P(None, 'wide'), may hold values from -3.140625 to 3.140625
- filter_mid: bfloat16 [2, 128, 128], P(None, 'wide'), may hold values from -0.5 to 0.5
- filter_mid_bias: bfloat16 [2, 128], P(None, 'wide'), may hold values from -3.140625 to 3.140625
- filter_out: bfloat16 [2, 128, 1536], P(None, None, 'wide'), may hold values from -0.5 to 0.5
- decay_rates: bfloat16 [2, 768], P(None, 'wide'), may hold values from 3 to 15
- out_right: bfloat16 [2, 768, 192], P(None, 'wide'), may hold values from -0.4375 to 0.4375
- out_left: bfloat16 [2, 768, 192], P(None, 'wide'), may hold values from -0.4375 to 0.4375
- glu_right: bfloat16 [2, 2, 768, 768], P(None, None, 'wide'), may hold values from -0.4375 to 0.4375
- glu_left: bfloat16 [2, 2, 3072, 768], P(None, None, 'wide'), may hold values from -0.21875 to 0.21875
- down_right: bfloat16 [2, 3072, 192], P(None, 'wide'), may hold values from -0.21875 to 0.21875
- down_left: bfloat16 [2, 768, 192], P(None, 'wide'), may hold values from -0.4375 to 0.4375
Outputs:
- output: bfloat16 [12288, 768], P(('wide', 'narrow'))
- grad_input: float32 [12288, 768], P(('wide', 'narrow'))
- grad_mask_vector: float32 [768], P('wide')
- grad_norm_gain: float32 [2, 2, 768], P(None, None, 'wide')
- grad_norm_bias: float32 [2, 2, 768], P(None, None, 'wide')
- grad_in_right: float32 [2, 2, 768, 192], P(None, None, 'wide')
- grad_in_left: float32 [2, 2, 768, 192], P(None, None, 'wide')
- grad_conv_taps: float32 [2, 3, 768], P(None, None, 'wide')
- grad_skip_bias: float32 [2, 768], P(None, 'wide')
- grad_filter_in: float32 [2, 5, 128], P(None, None, 'wide')
- grad_filter_in_bias: float32 [2, 128], P(None, 'wide')
- grad_filter_mid: float32 [2, 128, 128], P(None, 'wide')
- grad_filter_mid_bias: float32 [2, 128], P(None, 'wide')
- grad_filter_out: float32 [2, 128, 1536], P(None, None, 'wide')
- grad_out_right: float32 [2, 768, 192], P(None, 'wide')
- grad_out_left: float32 [2, 768, 192], P(None, 'wide')
- grad_glu_right: float32 [2, 2, 768, 768], P(None, None, 'wide')
- grad_glu_left: float32 [2, 2, 3072, 768], P(None, None, 'wide')
- grad_down_right: float32 [2, 3072, 192], P(None, 'wide')
- grad_down_left: float32 [2, 768, 192], P(None, 'wide')
Inputs may be any that keep to these rules, and one draw needn't show every extreme that they name: `mask_positions`: each row lists 38 different positions of its sequence.
All inputs are finite; a program needn't handle non-finite values.
Results may differ from a plain program's by a relative error of at most 0.024.
Values may be sent and summed in bfloat16 or wider, within the bound.
A program may use at most 320 MiB of HBM per device.

v0:
```python
from functools import partial
import math

import jax
import jax.numpy as jnp
from jax import lax
from jax.sharding import PartitionSpec as P

BLOCKS = 4
EMB = 5
LAYERS = 2


EPSILON = 1e-05
highest_precision = lax.Precision.HIGHEST


def permute(values):
    array_shape = values.shape
    blocks = array_shape[-2]
    split_view = values.reshape(array_shape[:-1] + (blocks, array_shape[-1] // blocks))
    return jnp.swapaxes(split_view, -3, -2).reshape(array_shape)


def monarch_forward(inputs, right_factor, left_factor):
    row_count = inputs.shape[0]
    right_blocks = right_factor.reshape(BLOCKS, -1, right_factor.shape[-1])
    left_blocks = left_factor.reshape(BLOCKS, -1, left_factor.shape[-1])
    middle = jnp.einsum(
        "rbi,bio->rbo",
        inputs.reshape(row_count, BLOCKS, -1),
        right_blocks,
        preferred_element_type=jnp.float32,
    )
    middle = permute(middle).astype(jnp.bfloat16)
    output = jnp.einsum("rbi,bio->rbo", middle, left_blocks, preferred_element_type=jnp.float32)
    return (middle, output.reshape(row_count, -1))


def monarch_backward(inputs, middle, right_factor, left_factor, grad_output):
    row_count = inputs.shape[0]
    right_blocks = right_factor.reshape(BLOCKS, -1, right_factor.shape[-1])
    left_blocks = left_factor.reshape(BLOCKS, -1, left_factor.shape[-1])
    grad_low = grad_output.astype(jnp.bfloat16).reshape(row_count, BLOCKS, -1)
    grad_left = jnp.einsum("rbi,rbo->bio", middle, grad_low, preferred_element_type=jnp.float32)
    grad_middle = jnp.einsum(
        "rbo,bio->rbi", grad_low, left_blocks, preferred_element_type=jnp.float32
    )
    grad_middle = permute(grad_middle).astype(jnp.bfloat16)
    input_blocks = inputs.reshape(row_count, BLOCKS, -1)
    grad_right = jnp.einsum(
        "rbi,rbo->bio", input_blocks, grad_middle, preferred_element_type=jnp.float32
    )
    grad_inputs = jnp.einsum(
        "rbo,bio->rbi", grad_middle, right_blocks, preferred_element_type=jnp.float32
    )
    return (
        grad_inputs.reshape(row_count, -1),
        grad_right.reshape(right_factor.shape),
        grad_left.reshape(left_factor.shape),
    )


def layer_norm(values, norm_gain, norm_bias):
    average = jnp.mean(values, axis=-1, keepdims=True)
    centred = values - average
    variance = jnp.mean(centred * centred, axis=-1, keepdims=True)
    return centred * lax.rsqrt(variance + EPSILON) * norm_gain + norm_bias


def position_features(length):
    positions = jnp.arange(length, dtype=jnp.float32)
    fraction = positions / length
    features = [fraction]
    for band_index in range(1, (EMB - 1) // 2 + 1):
        features.append(jnp.cos(2.0 * math.pi * band_index * fraction))
        features.append(jnp.sin(2.0 * math.pi * band_index * fraction))
    return jnp.stack(features, axis=1)


def make_filter(
    filter_in, filter_in_bias, filter_mid, filter_mid_bias, filter_out, decay_rates, length
):
    embedding = position_features(length)
    first_hidden = jnp.sin(
        jnp.dot(embedding, filter_in, precision=highest_precision) + filter_in_bias
    )
    second = jnp.sin(
        jnp.dot(first_hidden, filter_mid, precision=highest_precision) + filter_mid_bias
    )
    kernel = jnp.dot(second, filter_out, precision=highest_precision)
    fraction = jnp.arange(length, dtype=jnp.float32)[:, None] / length
    both_rates = jnp.concatenate([decay_rates, decay_rates])
    return kernel * jnp.exp(-fraction * both_rates[None, :])


def short_convolution(signal_rows, conv_taps):
    padded = jnp.pad(signal_rows, ((0, 0), (2, 0), (0, 0)))
    return (
        conv_taps[0] * padded[:, :-2]
        + conv_taps[1] * padded[:, 1:-1]
        + conv_taps[2] * padded[:, 2:]
    )


def spectral_tables(length, span):
    padded_length = 2 * length
    frequency = jnp.arange(length + 1, dtype=jnp.int32)
    places = jnp.arange(span, dtype=jnp.int32)
    phase_index = frequency[:, None] * places[None, :] % padded_length
    angles = phase_index.astype(jnp.float32) * (2.0 * math.pi / padded_length)
    ends = (frequency == 0) | (frequency == length)
    weights = jnp.where(ends, 1.0, 2.0).astype(jnp.float32) / padded_length
    return (jnp.cos(angles), jnp.sin(angles), weights)


def circular_kernel(kernel):
    width = kernel.shape[1] // 2
    forward_part = kernel[:, :width]
    reverse_part = kernel[:, width:]
    first_row = forward_part[:1] + reverse_part[:1]
    spacer = jnp.zeros((1, width), jnp.float32)
    return jnp.concatenate(
        [first_row, forward_part[1:], spacer, jnp.flip(reverse_part[1:], axis=0)], axis=0
    )


def long_convolution(signal_rows, kernel):
    length = signal_rows.shape[1]
    cosine_lookup, sine_lookup, weights = spectral_tables(length, length)
    kernel_cosine, kernel_sine, unused = spectral_tables(length, 2 * length)
    circular = circular_kernel(kernel)
    real_signal = jnp.einsum("ik,hkm->him", cosine_lookup, signal_rows, precision=highest_precision)
    imaginary_signal = -jnp.einsum(
        "ik,hkm->him", sine_lookup, signal_rows, precision=highest_precision
    )
    kernel_real = jnp.dot(kernel_cosine, circular, precision=highest_precision)
    kernel_imaginary = -jnp.dot(kernel_sine, circular, precision=highest_precision)
    real_product = real_signal * kernel_real - imaginary_signal * kernel_imaginary
    imaginary_product = real_signal * kernel_imaginary + imaginary_signal * kernel_real
    inverse_cosine_table = cosine_lookup * weights[:, None]
    inverse_sine_table = sine_lookup * weights[:, None]
    return jnp.einsum(
        "hp,ihj->ipj", inverse_cosine_table, real_product, precision=highest_precision
    ) - jnp.einsum(
        "hp,ihj->ipj", inverse_sine_table, imaginary_product, precision=highest_precision
    )


def mixer_piece(
    value_path,
    gate_path,
    conv_taps,
    skip_bias,
    filter_in,
    filter_in_bias,
    filter_mid,
    filter_mid_bias,
    filter_out,
    decay_rates,
    live_mask,
    share,
):
    length = live_mask.shape[1]
    kernel = make_filter(
        filter_in, filter_in_bias, filter_mid, filter_mid_bias, filter_out, decay_rates, length
    )
    signal_rows = value_path.reshape(live_mask.shape[0], length, -1) * live_mask
    signal_rows = short_convolution(signal_rows, conv_taps) * live_mask
    mixed_signal = long_convolution(signal_rows, kernel) + signal_rows * skip_bias
    return (mixed_signal.reshape(value_path.shape) * gate_path, share * jnp.sum(kernel * kernel))


def glu_piece(upper_branch, gate_branch):
    return jax.nn.gelu(gate_branch, approximate=False) * upper_branch


def small_weights(layer_weights):
    return tuple(
        (layer_weights[position].astype(jnp.float32) for position in (4, 5, 6, 7, 8, 9, 10))
    )


def forward_layer(hidden, layer_weights, live_mask):
    (
        norm_gain,
        norm_bias,
        in_right,
        in_left,
        conv_taps,
        skip_bias,
        filter_in,
        filter_in_bias,
        filter_mid,
        filter_mid_bias,
        filter_out,
        decay_rates,
        out_right,
        out_left,
        glu_right,
        glu_left,
        down_right,
        down_left,
    ) = layer_weights
    gains = norm_gain.astype(jnp.float32)
    biases = norm_bias.astype(jnp.float32)
    small = small_weights(layer_weights)
    normed = layer_norm(hidden, gains[0], biases[0]).astype(jnp.bfloat16)
    middle_value, value_path = monarch_forward(normed, in_right[0], in_left[0])
    middle_gate, gate_path = monarch_forward(normed, in_right[1], in_left[1])
    mixed_signal, unused = mixer_piece(
        value_path,
        gate_path,
        small[0],
        small[1],
        small[2],
        small[3],
        small[4],
        small[5],
        small[6],
        decay_rates.astype(jnp.float32),
        live_mask,
        0.0,
    )
    mixed_signal = mixed_signal.astype(jnp.bfloat16)
    middle_out, branch = monarch_forward(mixed_signal, out_right, out_left)
    middle_hidden = hidden + branch
    normed_two = layer_norm(middle_hidden, gains[1], biases[1]).astype(jnp.bfloat16)
    middle_up, upper_branch = monarch_forward(normed_two, glu_right[0], glu_left[0])
    middle_glu, gate_branch = monarch_forward(normed_two, glu_right[1], glu_left[1])
    glu_hidden = glu_piece(upper_branch, gate_branch).astype(jnp.bfloat16)
    middle_down, branch_two = monarch_forward(glu_hidden, down_right, down_left)
    saved = (
        hidden,
        normed,
        middle_value,
        value_path,
        middle_gate,
        gate_path,
        mixed_signal,
        middle_out,
        middle_hidden,
        normed_two,
        middle_up,
        upper_branch,
        middle_glu,
        gate_branch,
        glu_hidden,
        middle_down,
    )
    return (middle_hidden + branch_two, saved)


def backward_layer(grad_hidden, layer_weights, saved, live_mask, share):
    (
        norm_gain,
        norm_bias,
        in_right,
        in_left,
        conv_taps,
        skip_bias,
        filter_in,
        filter_in_bias,
        filter_mid,
        filter_mid_bias,
        filter_out,
        decay_rates,
        out_right,
        out_left,
        glu_right,
        glu_left,
        down_right,
        down_left,
    ) = layer_weights
    (
        hidden,
        normed,
        middle_value,
        value_path,
        middle_gate,
        gate_path,
        mixed_signal,
        middle_out,
        middle_hidden,
        normed_two,
        middle_up,
        upper_branch,
        middle_glu,
        gate_branch,
        glu_hidden,
        middle_down,
    ) = saved
    gains = norm_gain.astype(jnp.float32)
    biases = norm_bias.astype(jnp.float32)
    small = small_weights(layer_weights)
    grad_glu, grad_down_right, grad_down_left = monarch_backward(
        glu_hidden, middle_down, down_right, down_left, grad_hidden
    )
    unused, glu_pull = jax.vjp(glu_piece, upper_branch, gate_branch)
    grad_upper, grad_gate = glu_pull(grad_glu)
    grad_normed_up, grad_right_up, grad_left_up = monarch_backward(
        normed_two, middle_up, glu_right[0], glu_left[0], grad_upper
    )
    grad_normed_gate, grad_right_gate, grad_left_gate = monarch_backward(
        normed_two, middle_glu, glu_right[1], glu_left[1], grad_gate
    )
    unused, norm_pull = jax.vjp(layer_norm, middle_hidden, gains[1], biases[1])
    grad_middle, grad_gain_two, grad_bias_two = norm_pull(grad_normed_up + grad_normed_gate)
    grad_middle = grad_middle + grad_hidden
    grad_mixed, grad_out_right, grad_out_left = monarch_backward(
        mixed_signal, middle_out, out_right, out_left, grad_middle
    )
    mixer_local = partial(
        mixer_piece, decay_rates=decay_rates.astype(jnp.float32), live_mask=live_mask, share=share
    )
    unused, mixer_pull = jax.vjp(
        mixer_local,
        value_path,
        gate_path,
        small[0],
        small[1],
        small[2],
        small[3],
        small[4],
        small[5],
        small[6],
    )
    mixer_grads = mixer_pull((grad_mixed, jnp.ones((), jnp.float32)))
    grad_normed_value, grad_right_value, grad_left_value = monarch_backward(
        normed, middle_value, in_right[0], in_left[0], mixer_grads[0]
    )
    grad_normed_path, grad_right_path, grad_left_path = monarch_backward(
        normed, middle_gate, in_right[1], in_left[1], mixer_grads[1]
    )
    unused, norm_pull_one = jax.vjp(layer_norm, hidden, gains[0], biases[0])
    grad_before, grad_gain_one, grad_bias_one = norm_pull_one(grad_normed_value + grad_normed_path)
    grads = (
        jnp.stack([grad_gain_one, grad_gain_two]),
        jnp.stack([grad_bias_one, grad_bias_two]),
        jnp.stack([grad_right_value, grad_right_path]),
        jnp.stack([grad_left_value, grad_left_path]),
        mixer_grads[2],
        mixer_grads[3],
        mixer_grads[4],
        mixer_grads[5],
        mixer_grads[6],
        mixer_grads[7],
        mixer_grads[8],
        grad_out_right,
        grad_out_left,
        jnp.stack([grad_right_up, grad_right_gate]),
        jnp.stack([grad_left_up, grad_left_gate]),
        grad_down_right,
        grad_down_left,
    )
    return (grad_before + grad_middle, grads)


def fetch_layer(shards, layer_index):
    return (
        lax.all_gather(shards[0][layer_index], "wide", axis=1, tiled=True),
        lax.all_gather(shards[1][layer_index], "wide", axis=1, tiled=True),
        lax.all_gather(shards[2][layer_index], "wide", axis=1, tiled=True),
        lax.all_gather(shards[3][layer_index], "wide", axis=1, tiled=True),
        lax.all_gather(shards[4][layer_index], "wide", axis=1, tiled=True),
        lax.all_gather(shards[5][layer_index], "wide", axis=0, tiled=True),
        lax.all_gather(shards[6][layer_index], "wide", axis=1, tiled=True),
        lax.all_gather(shards[7][layer_index], "wide", axis=0, tiled=True),
        lax.all_gather(shards[8][layer_index], "wide", axis=0, tiled=True),
        lax.all_gather(shards[9][layer_index], "wide", axis=0, tiled=True),
        lax.all_gather(shards[10][layer_index], "wide", axis=1, tiled=True),
        lax.all_gather(shards[11][layer_index], "wide", axis=0, tiled=True),
        lax.all_gather(shards[12][layer_index], "wide", axis=0, tiled=True),
        lax.all_gather(shards[13][layer_index], "wide", axis=0, tiled=True),
        lax.all_gather(shards[14][layer_index], "wide", axis=1, tiled=True),
        lax.all_gather(shards[15][layer_index], "wide", axis=1, tiled=True),
        lax.all_gather(shards[16][layer_index], "wide", axis=0, tiled=True),
        lax.all_gather(shards[17][layer_index], "wide", axis=0, tiled=True),
    )


def scatter_upper(grads):
    return (
        lax.psum_scatter(grads[0], "wide", scatter_dimension=1, tiled=True),
        lax.psum_scatter(grads[1], "wide", scatter_dimension=1, tiled=True),
        lax.psum_scatter(grads[2], "wide", scatter_dimension=1, tiled=True),
        lax.psum_scatter(grads[3], "wide", scatter_dimension=1, tiled=True),
        lax.psum_scatter(grads[4], "wide", scatter_dimension=1, tiled=True),
        lax.psum_scatter(grads[5], "wide", scatter_dimension=0, tiled=True),
        lax.psum_scatter(grads[6], "wide", scatter_dimension=1, tiled=True),
        lax.psum_scatter(grads[7], "wide", scatter_dimension=0, tiled=True),
        lax.psum_scatter(grads[8], "wide", scatter_dimension=0, tiled=True),
        lax.psum_scatter(grads[9], "wide", scatter_dimension=0, tiled=True),
        lax.psum_scatter(grads[10], "wide", scatter_dimension=1, tiled=True),
        lax.psum_scatter(grads[11], "wide", scatter_dimension=0, tiled=True),
        lax.psum_scatter(grads[12], "wide", scatter_dimension=0, tiled=True),
        lax.psum_scatter(grads[13], "wide", scatter_dimension=1, tiled=True),
        lax.psum_scatter(grads[14], "wide", scatter_dimension=1, tiled=True),
        lax.psum_scatter(grads[15], "wide", scatter_dimension=0, tiled=True),
        lax.psum_scatter(grads[16], "wide", scatter_dimension=0, tiled=True),
    )


def scatter_lower(grads, mask_term):
    return (
        lax.psum_scatter(grads[0], "wide", scatter_dimension=1, tiled=True),
        lax.psum_scatter(grads[1], "wide", scatter_dimension=1, tiled=True),
        lax.psum_scatter(grads[2], "wide", scatter_dimension=1, tiled=True),
        lax.psum_scatter(grads[3], "wide", scatter_dimension=1, tiled=True),
        lax.psum_scatter(grads[4], "wide", scatter_dimension=1, tiled=True),
        lax.psum_scatter(grads[5], "wide", scatter_dimension=0, tiled=True),
        lax.psum_scatter(grads[6], "wide", scatter_dimension=1, tiled=True),
        lax.psum_scatter(grads[7], "wide", scatter_dimension=0, tiled=True),
        lax.psum_scatter(grads[8], "wide", scatter_dimension=0, tiled=True),
        lax.psum_scatter(grads[9], "wide", scatter_dimension=0, tiled=True),
        lax.psum_scatter(grads[10], "wide", scatter_dimension=1, tiled=True),
        lax.psum_scatter(grads[11], "wide", scatter_dimension=0, tiled=True),
        lax.psum_scatter(grads[12], "wide", scatter_dimension=0, tiled=True),
        lax.psum_scatter(grads[13], "wide", scatter_dimension=1, tiled=True),
        lax.psum_scatter(grads[14], "wide", scatter_dimension=1, tiled=True),
        lax.psum_scatter(grads[15], "wide", scatter_dimension=0, tiled=True),
        lax.psum_scatter(grads[16], "wide", scatter_dimension=0, tiled=True),
        lax.psum_scatter(mask_term, "wide", scatter_dimension=0, tiled=True),
    )


def narrow_total(parts):
    flattened = jnp.concatenate([member.reshape(-1) for member in parts])
    summed = lax.psum(flattened.astype(jnp.bfloat16), "narrow").astype(jnp.float32)
    result = []
    offset = 0
    for member in parts:
        result.append(summed[offset : offset + member.size].reshape(member.shape))
        offset = offset + member.size
    return result


def body(
    hidden_in,
    seq_lengths,
    mask_positions,
    mask_vector,
    cotangent,
    norm_gain,
    norm_bias,
    in_right,
    in_left,
    conv_taps,
    skip_bias,
    filter_in,
    filter_in_bias,
    filter_mid,
    filter_mid_bias,
    filter_out,
    decay_rates,
    out_right,
    out_left,
    glu_right,
    glu_left,
    down_right,
    down_left,
):
    row_count = hidden_in.shape[0]
    seq_count = seq_lengths.shape[0]
    length = row_count // seq_count
    places = jnp.arange(length, dtype=jnp.int32)
    live_mask = (places[None, :] < seq_lengths[:, None]).astype(jnp.float32)[:, :, None]
    marked = jnp.any(mask_positions[:, :, None] == places[None, None, :], axis=1).reshape(
        row_count, 1
    )
    gathered = (
        lax.all_gather(mask_vector, "wide", axis=0, tiled=True),
        lax.all_gather(norm_gain, "wide", axis=2, tiled=True),
        lax.all_gather(norm_bias, "wide", axis=2, tiled=True),
        lax.all_gather(in_right, "wide", axis=2, tiled=True),
        lax.all_gather(in_left, "wide", axis=2, tiled=True),
        lax.all_gather(conv_taps, "wide", axis=2, tiled=True),
        lax.all_gather(skip_bias, "wide", axis=1, tiled=True),
        lax.all_gather(filter_in, "wide", axis=2, tiled=True),
        lax.all_gather(filter_in_bias, "wide", axis=1, tiled=True),
        lax.all_gather(filter_mid, "wide", axis=1, tiled=True),
        lax.all_gather(filter_mid_bias, "wide", axis=1, tiled=True),
        lax.all_gather(filter_out, "wide", axis=2, tiled=True),
        lax.all_gather(decay_rates, "wide", axis=1, tiled=True),
        lax.all_gather(out_right, "wide", axis=1, tiled=True),
        lax.all_gather(out_left, "wide", axis=1, tiled=True),
        lax.all_gather(glu_right, "wide", axis=2, tiled=True),
        lax.all_gather(glu_left, "wide", axis=2, tiled=True),
        lax.all_gather(down_right, "wide", axis=1, tiled=True),
        lax.all_gather(down_left, "wide", axis=1, tiled=True),
    )
    hidden = jnp.where(
        marked, gathered[0].astype(jnp.float32)[None, :], hidden_in.astype(jnp.float32)
    )
    saved_layers = []
    for layer_index in range(LAYERS):
        layer_weights = tuple((member[layer_index] for member in gathered[1:]))
        hidden, saved = forward_layer(hidden, layer_weights, live_mask)
        saved_layers.append(saved)
    output = hidden.astype(jnp.bfloat16)
    shards = (
        norm_gain,
        norm_bias,
        in_right,
        in_left,
        conv_taps,
        skip_bias,
        filter_in,
        filter_in_bias,
        filter_mid,
        filter_mid_bias,
        filter_out,
        decay_rates,
        out_right,
        out_left,
        glu_right,
        glu_left,
        down_right,
        down_left,
    )
    share = 0.5 * seq_count
    grad_hidden = cotangent.astype(jnp.float32)
    layer_grads = [None] * LAYERS
    mask_grad = None
    for layer_index in reversed(range(LAYERS)):
        layer_weights = fetch_layer(shards, layer_index)
        grad_hidden, grads = backward_layer(
            grad_hidden, layer_weights, saved_layers[layer_index], live_mask, share
        )
        if layer_index > 0:
            layer_grads[layer_index] = narrow_total(scatter_upper(grads))
        else:
            mask_term = jnp.sum(jnp.where(marked, grad_hidden, 0.0), axis=0)
            reduced = narrow_total(scatter_lower(grads, mask_term))
            layer_grads[0] = reduced[:-1]
            mask_grad = reduced[-1]
    final_grads = [
        jnp.stack([layer_grads[position][member_index] for position in range(LAYERS)])
        for member_index in range(17)
    ]
    grad_input = jnp.where(marked, 0.0, grad_hidden)
    return (output, grad_input, mask_grad) + tuple(final_grads)


def solution(mesh):
    placed = (
        P(("wide", "narrow"), None),
        P(("wide", "narrow")),
        P(("wide", "narrow"), None),
        P("wide"),
        P(("wide", "narrow"), None),
        P(None, None, "wide"),
        P(None, None, "wide"),
        P(None, None, "wide", None),
        P(None, None, "wide", None),
        P(None, None, "wide"),
        P(None, "wide"),
        P(None, None, "wide"),
        P(None, "wide"),
        P(None, "wide", None),
        P(None, "wide"),
        P(None, None, "wide"),
        P(None, "wide"),
        P(None, "wide", None),
        P(None, "wide", None),
        P(None, None, "wide", None),
        P(None, None, "wide", None),
        P(None, "wide", None),
        P(None, "wide", None),
    )
    return jax.shard_map(
        body,
        mesh=mesh,
        in_specs=placed,
        out_specs=(
            P(("wide", "narrow"), None),
            P(("wide", "narrow"), None),
            P("wide"),
            P(None, None, "wide"),
            P(None, None, "wide"),
            P(None, None, "wide", None),
            P(None, None, "wide", None),
            P(None, None, "wide"),
            P(None, "wide"),
            P(None, None, "wide"),
            P(None, "wide"),
            P(None, "wide", None),
            P(None, "wide"),
            P(None, None, "wide"),
            P(None, "wide", None),
            P(None, "wide", None),
            P(None, None, "wide", None),
            P(None, None, "wide", None),
            P(None, "wide", None),
            P(None, "wide", None),
        ),
        check_vma=False,
    )
```

profile of v0, /device:TPU:0, one launch (start us, length us, event | category | flops | bytes accessed | tf_op | source)
XLA Modules:
  0.0 4395.7 jit_solution(2190898557301985667)
XLA Ops:
  775.4 66.1 %all-gather.18 = bf16[1,768,192]{2,1,0:T(8,128)(2,1)} all-gather(bf16[1,96,192]{2,1,0:T(8,128)(2,1)S(1)} %copy-done.239), channel_id=20, replica_groups=mesh['wide'=8,'narrow'=4] {'wide'}, dimensions={1}, use_global_device_ids=true | all-gather | bytes 331776 | tf_op jit(solution)/shard_map/all_gather | solution.py:378
  972.9 45.3 %all_gather.173 = bf16[2,768,192]{2,1,0:T(8,128)(2,1)S(1)} all-gather(bf16[2,96,192]{2,1,0:T(8,128)(2,1)S(1)} %copy-done.209), channel_id=1, replica_groups=mesh['wide'=8,'narrow'=4] {'wide'}, dimensions={1}, use_global_device_ids=true | all-gather | bytes 663552 | tf_op jit(solution)/shard_map/all_gather | solution.py:486
  1019.1 48.0 %all_gather.172 = bf16[2,768,192]{2,1,0:T(8,128)(2,1)S(1)} all-gather(bf16[2,96,192]{2,1,0:T(8,128)(2,1)S(1)} %copy-done.210), channel_id=1, replica_groups=mesh['wide'=8,'narrow'=4] {'wide'}, dimensions={1}, use_global_device_ids=true | all-gather | bytes 663552 | tf_op jit(solution)/shard_map/all_gather | solution.py:485
  1069.7 47.7 %all_gather.177 = bf16[2,768,192]{2,1,0:T(8,128)(2,1)S(1)} all-gather(bf16[2,96,192]{2,1,0:T(8,128)(2,1)S(1)} %copy-done.212), channel_id=1, replica_groups=mesh['wide'=8,'narrow'=4] {'wide'}, dimensions={1}, use_global_device_ids=true | all-gather | bytes 663552 | tf_op jit(solution)/shard_map/all_gather | solution.py:490
  1118.3 46.7 %all-gather.17 = bf16[1,2,768,192]{3,2,1,0:T(8,128)(2,1)S(1)} all-gather(bf16[1,2,96,192]{3,2,1,0:T(8,128)(2,1)S(1)} %get-tuple-element.334), channel_id=19, replica_groups=mesh['wide'=8,'narrow'=4] {'wide'}, dimensions={2}, use_global_device_ids=true | all-gather | bytes 663552 | tf_op jit(solution)/shard_map/all_gather | solution.py:363
  1885.5 57.8 %reduce-scatter.85.cloned.1.call-done = f32[96,2]{1,0:T(8,128)} async-done(((f32[768,2]{1,0:T(8,128)}), f32[96,2]{1,0:T(8,128)}) %reduce-scatter.85.cloned.1.call-update) | async-done | bytes 784
  1944.8 62.7 %reduce-scatter.87.cloned.1.call-done = f32[96,2]{1,0:T(8,128)} async-done(((f32[768,2]{1,0:T(8,128)}), f32[96,2]{1,0:T(8,128)}) %reduce-scatter.87.cloned.1.call-update) | async-done | bytes 784
  2008.9 62.1 %reduce-scatter.93.cloned.1.call-done = f32[96,2]{1,0:T(8,128)} async-done(((f32[768,2]{1,0:T(8,128)}), f32[96,2]{1,0:T(8,128)}) %reduce-scatter.93.cloned.1.call-update) | async-done | bytes 784
  2072.5 62.1 %reduce-scatter.95.cloned.1.call-done = f32[96,2]{1,0:T(8,128)} async-done(((f32[768,2]{1,0:T(8,128)}), f32[96,2]{1,0:T(8,128)}) %reduce-scatter.95.cloned.1.call-update) | async-done | bytes 784
  2136.1 62.1 %reduce-scatter.89.cloned.1.call-done = f32[96,3]{1,0:T(8,128)} async-done(((f32[768,3]{1,0:T(8,128)}), f32[96,3]{1,0:T(8,128)}) %reduce-scatter.89.cloned.1.call-update) | async-done | bytes 1168
  2199.2 62.8 %reduce-scatter.97.cloned.1.call-done = f32[96,3]{1,0:T(8,128)} async-done(((f32[768,3]{1,0:T(8,128)}), f32[96,3]{1,0:T(8,128)}) %reduce-scatter.97.cloned.1.call-update) | async-done | bytes 1168
  2263.5 62.6 %reduce-scatter.49.cloned.1.call-done = f32[16,128]{1,0:T(8,128)} async-done(((f32[128,128]{1,0:T(8,128)}), f32[16,128]{1,0:T(8,128)}) %reduce-scatter.49.cloned.1.call-update) | async-done | bytes 8208 | tf_op jit(solution)/shard_map/reduce_scatter | solution.py:414
  2326.8 63.0 %reduce-scatter.69.cloned.1.call-done = f32[16,128]{1,0:T(8,128)} async-done(((f32[128,128]{1,0:T(8,128)}), f32[16,128]{1,0:T(8,128)}) %reduce-scatter.69.cloned.1.call-update) | async-done | bytes 8208 | tf_op jit(solution)/shard_map/reduce_scatter | solution.py:392
  2390.4 64.1 %reduce-scatter.53.cloned.1.call-done = f32[96,192]{1,0:T(8,128)} async-done(((f32[768,192]{1,0:T(8,128)}), f32[96,192]{1,0:T(8,128)}) %reduce-scatter.53.cloned.1.call-update) | async-done | bytes 73744 | tf_op jit(solution)/shard_map/reduce_scatter | solution.py:417
  2456.2 63.4 %reduce-scatter.55.cloned.1.call-done = f32[96,192]{1,0:T(8,128)} async-done(((f32[768,192]{1,0:T(8,128)}), f32[96,192]{1,0:T(8,128)}) %reduce-scatter.55.cloned.1.call-update) | async-done | bytes 73744 | tf_op jit(solution)/shard_map/reduce_scatter | solution.py:418
  2521.2 63.0 %reduce-scatter.63.cloned.1.call-done = f32[96,192]{1,0:T(8,128)} async-done(((f32[768,192]{1,0:T(8,128)}), f32[96,192]{1,0:T(8,128)}) %reduce-scatter.63.cloned.1.call-update) | async-done | bytes 73744 | tf_op jit(solution)/shard_map/reduce_scatter | solution.py:422
  2585.9 63.5 %reduce-scatter.73.cloned.1.call-done = f32[96,192]{1,0:T(8,128)} async-done(((f32[768,192]{1,0:T(8,128)}), f32[96,192]{1,0:T(8,128)}) %reduce-scatter.73.cloned.1.call-update) | async-done | bytes 73744 | tf_op jit(solution)/shard_map/reduce_scatter | solution.py:395
  2651.0 62.9 %reduce-scatter.75.cloned.1.call-done = f32[96,192]{1,0:T(8,128)} async-done(((f32[768,192]{1,0:T(8,128)}), f32[96,192]{1,0:T(8,128)}) %reduce-scatter.75.cloned.1.call-update) | async-done | bytes 73744 | tf_op jit(solution)/shard_map/reduce_scatter | solution.py:396
  2715.6 63.4 %reduce-scatter.83.cloned.1.call-done = f32[96,192]{1,0:T(8,128)} async-done(((f32[768,192]{1,0:T(8,128)}), f32[96,192]{1,0:T(8,128)}) %reduce-scatter.83.cloned.1.call-update) | async-done | bytes 73744 | tf_op jit(solution)/shard_map/reduce_scatter | solution.py:400
  2780.6 63.1 %reduce-scatter.51.cloned.1.call-done = f32[128,192]{0,1:T(8,128)} async-done(((f32[128,1536]{0,1:T(8,128)}), f32[128,192]{0,1:T(8,128)}) %reduce-scatter.51.cloned.1.call-update) | async-done | bytes 98320 | tf_op jit(solution)/shard_map/reduce_scatter | solution.py:416
  2845.5 63.3 %reduce-scatter.71.cloned.1.call-done = f32[128,192]{0,1:T(8,128)} async-done(((f32[128,1536]{0,1:T(8,128)}), f32[128,192]{0,1:T(8,128)}) %reduce-scatter.71.cloned.1.call-update) | async-done | bytes 98320 | tf_op jit(solution)/shard_map/reduce_scatter | solution.py:394
  2910.6 65.4 %reduce-scatter.45.cloned.1.call-done = f32[2,96,192]{2,1,0:T(8,128)} async-done(((f32[2,768,192]{2,1,0:T(8,128)}), f32[2,96,192]{2,1,0:T(8,128)}) %reduce-scatter.45.cloned.1.call-update) | async-done | bytes 147472 | tf_op jit(solution)/shard_map/reduce_scatter | solution.py:408
  2977.8 65.9 %reduce-scatter.47.cloned.1.call-done = f32[2,96,192]{2,1,0:T(8,128)} async-done(((f32[2,768,192]{2,1,0:T(8,128)}), f32[2,96,192]{2,1,0:T(8,128)}) %reduce-scatter.47.cloned.1.call-update) | async-done | bytes 147472 | tf_op jit(solution)/shard_map/reduce_scatter | solution.py:409
  3045.4 65.5 %reduce-scatter.65.cloned.1.call-done = f32[2,96,192]{2,1,0:T(8,128)} async-done(((f32[2,768,192]{2,1,0:T(8,128)}), f32[2,96,192]{2,1,0:T(8,128)}) %reduce-scatter.65.cloned.1.call-update) | async-done | bytes 147472 | tf_op jit(solution)/shard_map/reduce_scatter | solution.py:386
  3112.6 65.8 %reduce-scatter.67.cloned.1.call-done = f32[2,96,192]{2,1,0:T(8,128)} async-done(((f32[2,768,192]{2,1,0:T(8,128)}), f32[2,96,192]{2,1,0:T(8,128)}) %reduce-scatter.67.cloned.1.call-update) | async-done | bytes 147472 | tf_op jit(solution)/shard_map/reduce_scatter | solution.py:387
  3180.1 69.7 %reduce-scatter.61.cloned.1.call-done = f32[384,192]{0,1:T(8,128)} async-done(((f32[3072,192]{0,1:T(8,128)}), f32[384,192]{0,1:T(8,128)}) %reduce-scatter.61.cloned.1.call-update) | async-done | bytes 294928 | tf_op jit(solution)/shard_map/reduce_scatter | solution.py:421
  3251.9 69.6 %reduce-scatter.81.cloned.1.call-done = f32[384,192]{0,1:T(8,128)} async-done(((f32[3072,192]{0,1:T(8,128)}), f32[384,192]{0,1:T(8,128)}) %reduce-scatter.81.cloned.1.call-update) | async-done | bytes 294928 | tf_op jit(solution)/shard_map/reduce_scatter | solution.py:399
  3323.5 96.5 %reduce-scatter.57.cloned.1.call-done = f32[2,96,768]{2,1,0:T(8,128)} async-done(((f32[2,768,768]{2,1,0:T(8,128)}), f32[2,96,768]{2,1,0:T(8,128)}) %reduce-scatter.57.cloned.1.call-update) | async-done | bytes 589840 | tf_op jit(solution)/shard_map/reduce_scatter | solution.py:419
  3422.1 96.7 %reduce-scatter.77.cloned.1.call-done = f32[2,96,768]{2,1,0:T(8,128)} async-done(((f32[2,768,768]{2,1,0:T(8,128)}), f32[2,96,768]{2,1,0:T(8,128)}) %reduce-scatter.77.cloned.1.call-update) | async-done | bytes 589840 | tf_op jit(solution)/shard_map/reduce_scatter | solution.py:397
  3520.8 314.9 %reduce-scatter.59.cloned.1.call-done = f32[2,384,768]{2,1,0:T(8,128)} async-done(((f32[2,3072,768]{2,1,0:T(8,128)}), f32[2,384,768]{2,1,0:T(8,128)}) %reduce-scatter.59.cloned.1.call-update) | async-done | bytes 2359312 | tf_op jit(solution)/shard_map/reduce_scatter | solution.py:420
  3838.5 313.4 %reduce-scatter.79.cloned.1.call-done = f32[2,384,768]{2,1,0:T(8,128)} async-done(((f32[2,3072,768]{2,1,0:T(8,128)}), f32[2,384,768]{2,1,0:T(8,128)}) %reduce-scatter.79.cloned.1.call-update) | async-done | bytes 2359312 | tf_op jit(solution)/shard_map/reduce_scatter | solution.py:398
  4234.5 76.5 %all-reduce.43.cloned.1.call-done = (bf16[967632]{0:T(1024)(128)(2,1)}, bf16[967536]{0:T(1024)(128)(2,1)}) async-done(((bf16[967632]{0:T(1024)(128)(2,1)}, bf16[967536]{0:T(1024)(128)(2,1)}), (bf16[967632]{0:T(1024)(128)(2,1)}, bf16[967536]{0:T(1024)(128)(2,1)})) %all-reduce.43.cloned.1.call-update) | async-done | bytes 3870352 | tf_op jit(solution)/shard_map/psum | solution.py:429
  (1417 shorter events, 1818.0 us)
Async XLA Ops:
  7.2 1302.8 %all-gather.50.cloned.1.call-start = ((), (), s32[]{:S(2)}) async-start(), calls=%async_computation.28 | async-start | bytes 1769472 | tf_op jit(solution)/shard_map/all_gather | solution.py:475
  7.9 1305.1 %all-gather.52.cloned.1.call-start = ((), (), s32[]{:S(2)}) async-start(), calls=%async_computation.29 | async-start | bytes 1769472 | tf_op jit(solution)/shard_map/all_gather | solution.py:476
  8.7 1330.2 %all-gather.60.cloned.1.call-start = ((), (), s32[]{:S(2)}) async-start(), calls=%async_computation.53 | async-start | bytes 1327104 | tf_op jit(solution)/shard_map/all_gather | solution.py:377
  10.5 1331.4 %all-gather.66.cloned.1.call-start = ((), (), s32[]{:S(2)}) async-start(), calls=%async_computation.56 | async-start | bytes 1327104 | tf_op jit(solution)/shard_map/all_gather | solution.py:377
  11.1 1339.3 %all-gather.58.cloned.1.call-start = ((), (), s32[]{:S(2)}) async-start(), calls=%async_computation.32 | async-start | bytes 2654208 | tf_op jit(solution)/shard_map/all_gather | solution.py:489
  11.7 1346.6 %all-gather.64.cloned.1.call-start = ((), (), s32[]{:S(2)}) async-start(), calls=%async_computation.55 | async-start | bytes 2654208 | tf_op jit(solution)/shard_map/all_gather | solution.py:375
  12.6 1348.9 %all-gather.70.cloned.1.call-start = ((), (), s32[]{:S(2)}) async-start(), calls=%async_computation.58 | async-start | bytes 2654208 | tf_op jit(solution)/shard_map/all_gather | solution.py:375
  13.4 1351.3 %all-gather.54.cloned.1.call-start = ((), (), s32[]{:S(2)}) async-start(), calls=%async_computation.30 | async-start | bytes 5308416 | tf_op jit(solution)/shard_map/all_gather | solution.py:487
  14.1 1374.6 %all-gather.62.cloned.1.call-start = ((), (), s32[]{:S(2)}) async-start(), calls=%async_computation.54 | async-start | bytes 10616832 | tf_op jit(solution)/shard_map/all_gather | solution.py:376
  15.8 1380.9 %all-gather.68.cloned.1.call-start = ((), (), s32[]{:S(2)}) async-start(), calls=%async_computation.57 | async-start | bytes 10616832 | tf_op jit(solution)/shard_map/all_gather | solution.py:376
  16.4 1388.2 %all-gather.56.cloned.1.call-start = ((), (), s32[]{:S(2)}) async-start(), calls=%async_computation.31 | async-start | bytes 21233664 | tf_op jit(solution)/shard_map/all_gather | solution.py:488
  17.1 1865.6 %reduce-scatter.91.cloned.1.call-start = ((), (), s32[]{:S(2)}) async-start(), calls=%async_computation.62 | async-start | bytes 73728
  1749.6 640.2 %reduce-scatter.69.cloned.1.call-start = ((), (), s32[]{:S(2)}) async-start(), calls=%async_computation.45 | async-start | bytes 73728 | tf_op jit(solution)/shard_map/reduce_scatter | solution.py:392
  1751.4 703.1 %reduce-scatter.53.cloned.1.call-start = ((), (), s32[]{:S(2)}) async-start(), calls=%async_computation.37 | async-start | bytes 884736 | tf_op jit(solution)/shard_map/reduce_scatter | solution.py:417
  1753.8 765.8 %reduce-scatter.55.cloned.1.call-start = ((), (), s32[]{:S(2)}) async-start(), calls=%async_computation.38 | async-start | bytes 884736 | tf_op jit(solution)/shard_map/reduce_scatter | solution.py:418
  1756.5 827.7 %reduce-scatter.63.cloned.1.call-start = ((), (), s32[]{:S(2)}) async-start(), calls=%async_computation.42 | async-start | bytes 884736 | tf_op jit(solution)/shard_map/reduce_scatter | solution.py:422
  1759.0 890.4 %reduce-scatter.73.cloned.1.call-start = ((), (), s32[]{:S(2)}) async-start(), calls=%async_computation.47 | async-start | bytes 884736 | tf_op jit(solution)/shard_map/reduce_scatter | solution.py:395
  1761.7 952.3 %reduce-scatter.75.cloned.1.call-start = ((), (), s32[]{:S(2)}) async-start(), calls=%async_computation.48 | async-start | bytes 884736 | tf_op jit(solution)/shard_map/reduce_scatter | solution.py:396
  1764.1 1014.9 %reduce-scatter.83.cloned.1.call-start = ((), (), s32[]{:S(2)}) async-start(), calls=%async_computation.52 | async-start | bytes 884736 | tf_op jit(solution)/shard_map/reduce_scatter | solution.py:400
  1766.6 1077.1 %reduce-scatter.51.cloned.1.call-start = ((), (), s32[]{:S(2)}) async-start(), calls=%async_computation.36 | async-start | bytes 884736 | tf_op jit(solution)/shard_map/reduce_scatter | solution.py:416
  1770.2 1138.7 %reduce-scatter.71.cloned.1.call-start = ((), (), s32[]{:S(2)}) async-start(), calls=%async_computation.46 | async-start | bytes 884736 | tf_op jit(solution)/shard_map/reduce_scatter | solution.py:394
  1773.6 1202.5 %reduce-scatter.45.cloned.1.call-start = ((), (), s32[]{:S(2)}) async-start(), calls=%async_computation.33 | async-start | bytes 1769472 | tf_op jit(solution)/shard_map/reduce_scatter | solution.py:408
  1776.3 1267.3 %reduce-scatter.47.cloned.1.call-start = ((), (), s32[]{:S(2)}) async-start(), calls=%async_computation.34 | async-start | bytes 1769472 | tf_op jit(solution)/shard_map/reduce_scatter | solution.py:409
  1779.6 1331.2 %reduce-scatter.65.cloned.1.call-start = ((), (), s32[]{:S(2)}) async-start(), calls=%async_computation.43 | async-start | bytes 1769472 | tf_op jit(solution)/shard_map/reduce_scatter | solution.py:386
  1783.0 1395.4 %reduce-scatter.67.cloned.1.call-start = ((), (), s32[]{:S(2)}) async-start(), calls=%async_computation.44 | async-start | bytes 1769472 | tf_op jit(solution)/shard_map/reduce_scatter | solution.py:387
  1786.3 1463.5 %reduce-scatter.61.cloned.1.call-start = ((), (), s32[]{:S(2)}) async-start(), calls=%async_computation.41 | async-start | bytes 2654208 | tf_op jit(solution)/shard_map/reduce_scatter | solution.py:421
  1790.0 1531.4 %reduce-scatter.81.cloned.1.call-start = ((), (), s32[]{:S(2)}) async-start(), calls=%async_computation.51 | async-start | bytes 2654208 | tf_op jit(solution)/shard_map/reduce_scatter | solution.py:399
  1794.1 1625.9 %reduce-scatter.57.cloned.1.call-start = ((), (), s32[]{:S(2)}) async-start(), calls=%async_computation.39 | async-start | bytes 5308416 | tf_op jit(solution)/shard_map/reduce_scatter | solution.py:419
  1800.9 1717.8 %reduce-scatter.77.cloned.1.call-start = ((), (), s32[]{:S(2)}) async-start(), calls=%async_computation.49 | async-start | bytes 5308416 | tf_op jit(solution)/shard_map/reduce_scatter | solution.py:397
  1807.9 2027.8 %reduce-scatter.59.cloned.1.call-start = ((), (), s32[]{:S(2)}) async-start(), calls=%async_computation.40 | async-start | bytes 21233664 | tf_op jit(solution)/shard_map/reduce_scatter | solution.py:420
  1823.3 2328.6 %reduce-scatter.79.cloned.1.call-start = ((), (), s32[]{:S(2)}) async-start(), calls=%async_computation.50 | async-start | bytes 21233664 | tf_op jit(solution)/shard_map/reduce_scatter | solution.py:398
  1838.8 2472.2 %all-reduce.43.cloned.1.call-start = ((), (), s32[]{:S(2)}) async-start(), calls=%async_computation.67 | async-start | bytes 7741440 | tf_op jit(solution)/shard_map/psum | solution.py:429
  (384 other events, 13920.7 us)
Sparse Core Ops, SparseCore 0:
  369.2 84.6 all-gather.53
  456.2 154.5 all-gather.61
  612.8 155.6 all-gather.67
  770.1 463.0 all-gather.55
  1728.2 86.5 reduce-scatter.90
  1818.8 60.2 reduce-scatter.98
  1882.8 60.4 reduce-scatter.84
  1947.0 60.4 reduce-scatter.86
  2010.6 60.3 reduce-scatter.92
  2074.1 60.4 reduce-scatter.94
  2137.7 60.4 reduce-scatter.88
  2201.5 60.4 reduce-scatter.96
  2265.7 60.2 reduce-scatter.48
  2393.0 61.4 reduce-scatter.52
  2458.2 61.3 reduce-scatter.54
  2522.8 61.4 reduce-scatter.62
  2587.9 61.4 reduce-scatter.72
  2652.6 61.3 reduce-scatter.74
  2717.5 61.4 reduce-scatter.82
  2782.3 61.4 reduce-scatter.50
  2847.4 61.3 reduce-scatter.70
  2912.1 63.8 reduce-scatter.44
  2979.9 63.7 reduce-scatter.46
  3047.1 63.7 reduce-scatter.64
  3114.5 63.7 reduce-scatter.66
  3181.8 67.9 reduce-scatter.60
  3253.3 68.0 reduce-scatter.80
  3325.5 94.4 reduce-scatter.56
  3423.5 95.1 reduce-scatter.76
  3522.6 313.0 reduce-scatter.58
  3839.4 312.4 reduce-scatter.78
  4231.1 79.8 all-reduce.42
  (8 shorter events, 402.9 us)
where the time goes:
time: 4410 us; the launch traced here: 4400 us
  waiting for transfers between devices  2310 us (52%)
  blocking collectives  1200 us (27%)
  local copies, waits for them, and re-layouts  477 us (11%)
  matrix products  278 us (6%)
  other arithmetic  108 us (2%)
    unnamed x48, waiting for transfers between devices  375 us
    reduce_scatter x1, waiting for transfers between devices, scatter_lower(): lax.psum_scatter(grads[14], 'wide', scatter_dimension=1, tiled=True)  315 us
    reduce_scatter x1, waiting for transfers between devices, scatter_upper(): lax.psum_scatter(grads[14], 'wide', scatter_dimension=1, tiled=True)  313 us
    all_gather x2, blocking collectives, fetch_layer(): lax.all_gather(shards[17][layer_index], 'wide', axis=0, tiled=True)  99.7 us
    reduce_scatter x1, waiting for transfers between devices, scatter_upper(): lax.psum_scatter(grads[13], 'wide', scatter_dimension=1, tiled=True)  96.7 us
    reduce_scatter x1, waiting for transfers between devices, scatter_lower(): lax.psum_scatter(grads[13], 'wide', scatter_dimension=1, tiled=True)  96.5 us
  transfers between devices with their start and end apart: 40, of which 27 were waited for; matrix products, arithmetic and copies ran while one was open for 8% of the time, Pallas kernels for 0%

commit v1 on v0

--- a/solution.py
+++ b/solution.py
@@ -3,7 +3,10 @@
 
 import jax
 import jax.numpy as jnp
+import numpy as np
 from jax import lax
+from jax.experimental import pallas as pl
+from jax.experimental.pallas import tpu as pltpu
 from jax.sharding import PartitionSpec as P
 
 BLOCKS = 4
@@ -356,71 +359,954 @@
     return (grad_before + grad_middle, grads)
 
 
-def fetch_layer(shards, layer_index):
+F32 = jnp.float32
+BF16 = jnp.bfloat16
+VMEM_BYTES = 60 * 1024 * 1024
+
+
+def dot(left, right):
+    return jnp.dot(left, right, preferred_element_type=F32)
+
+
+def dot_rows(left, right):
+    return lax.dot_general(left, right, (((0,), (0,)), ((), ())), preferred_element_type=F32)
+
+
+def dot_columns(left, right):
+    return lax.dot_general(left, right, (((1,), (1,)), ((), ())), preferred_element_type=F32)
+
+
+def exact(left, right, dims=(1, 0)):
+    return lax.dot_general(
+        left,
+        right,
+        (((dims[0],), (dims[1],)), ((), ())),
+        precision=highest_precision,
+        preferred_element_type=F32,
+    )
+
+
+def columns(values, index, width):
+    return values[:, index * width : (index + 1) * width]
+
+
+def shuffled(parts):
+    chunk = parts[0].shape[1] // BLOCKS
+    return [
+        jnp.concatenate([columns(part, index, chunk) for part in parts], axis=1)
+        for index in range(BLOCKS)
+    ]
+
+
+def normalised(values):
+    average = jnp.mean(values, axis=-1, keepdims=True)
+    centred = values - average
+    variance = jnp.mean(centred * centred, axis=-1, keepdims=True)
+    scale = lax.rsqrt(variance + EPSILON)
+    return centred * scale, scale
+
+
+def norm_backward(grad, hidden, gain):
+    unit, scale = normalised(hidden)
+    grad_gain = jnp.sum(grad * unit, axis=0, keepdims=True)
+    grad_bias = jnp.sum(grad, axis=0, keepdims=True)
+    scaled = grad * gain
+    mean_one = jnp.mean(scaled, axis=-1, keepdims=True)
+    mean_two = jnp.mean(scaled * unit, axis=-1, keepdims=True)
+    return scale * (scaled - mean_one - unit * mean_two), grad_gain, grad_bias
+
+
+def flip(bit, by):
+    return 1 - bit if by else bit
+
+
+def place():
+    w = lax.axis_index("wide")
+    n = lax.axis_index("narrow")
+    return w // 2, w % 2, n // 2, n % 2
+
+
+KINDS = ((0, 0, 0, 4), (1, 0, 0, 4), (0, 1, 0, 4), (1, 1, 0, 2), (1, 1, 2, 2))
+
+
+def relative(z, distance):
+    high, low = z // 2, z % 2
+    return 2 * flip(high, distance // 2) + flip(low, distance % 2)
+
+
+def piece_copies(pieces, sems, targets_of):
+    z, x, y, c = place()
+    copies = []
+    for core in range(2):
+        for kind, (dx, dy, first, count) in enumerate(KINDS):
+            source = pieces[core * len(KINDS) + kind]
+            for slot in range(count):
+                owner = (relative(z, first + slot), flip(x, dx), flip(y, dy), flip(c, core))
+                for row, target in targets_of(*owner):
+                    view = source.at[slot, pl.ds(row, target.shape[0])]
+                    copies.append(pltpu.make_async_copy(view, target, sems.at[len(copies)]))
+    return copies
+
+
+def grad_copies(result, sems, sources_of):
+    z, x, y, c = place()
+    copies = []
+    for core in range(2):
+        for dx in range(2):
+            for dy in range(2):
+                for dz in range(4):
+                    owner = (relative(z, dz), flip(x, dx), flip(y, dy), flip(c, core))
+                    for row, source in sources_of(*owner):
+                        view = result.at[core, dx, dy, dz, pl.ds(row, source.shape[0])]
+                        copies.append(pltpu.make_async_copy(source, view, sems.at[len(copies)]))
+    return copies
+
+
+def start_all(copies):
+    for copy in copies:
+        copy.start()
+
+
+def wait_all(copies):
+    for copy in copies:
+        copy.wait()
+
+
+def glu_spots(left, right):
+    def spots(z, x, y, c):
+        tall, short = left.shape[2] // 4, right.shape[1] // 16
+        return (
+            (0, left.at[y, z, pl.ds(pl.multiple_of((2 * x + c) * tall, 16), tall)]),
+            (tall, right.at[y, pl.ds(pl.multiple_of((4 * z + 2 * x + c) * short, 16), short)]),
+        )
+
+    return spots
+
+
+def mix_spots(mix):
+    def spots(z, x, y, c):
+        rows = mix.shape[1] // 4
+        return ((0, mix.at[2 * z + x, pl.ds(pl.multiple_of((2 * y + c) * rows, 16), rows)]),)
+
+    return spots
+
+
+def factor(mix, rows, kind, block):
+    width = mix.shape[2] // 4
+    low = kind * width
+    top = mix[2 * block, rows : rows + width // 2, low : low + width]
+    bottom = mix[2 * block + 1, rows : rows + width // 2, low : low + width]
+    return jnp.concatenate([top, bottom], axis=0)
+
+
+def down_factor(mix, first, block):
+    width = mix.shape[2] // 4
+    half = width // 2
+    parts = []
+    for shard in (2 * block, 2 * block + 1):
+        for index in range(4):
+            parts.append(mix[shard, first : first + half, index * width : (index + 1) * width])
+    return jnp.concatenate(parts, axis=0)
+
+
+def monarch_small(inputs, right, left):
+    width = inputs.shape[1] // BLOCKS
+    parts = [dot(columns(inputs, b, width), right(b)) for b in range(BLOCKS)]
+    middle = [part.astype(BF16) for part in shuffled(parts)]
+    return middle, [dot(middle[b], left(b)) for b in range(BLOCKS)]
+
+
+def monarch_small_backward(inputs, middle, grads, right, left):
+    width = inputs.shape[1] // BLOCKS
+    grad_left = [dot_rows(middle[b], grads[b]) for b in range(BLOCKS)]
+    back = shuffled([dot_columns(grads[b], left(b)) for b in range(BLOCKS)])
+    back = [part.astype(BF16) for part in back]
+    grad_right = [dot_rows(columns(inputs, b, width), back[b]) for b in range(BLOCKS)]
+    return [dot_columns(back[b], right(b)) for b in range(BLOCKS)], grad_right, grad_left
+
+
+def store_factor(mix, rows, kind, block, value):
+    width = mix.shape[2] // 4
+    half = width // 2
+    low = kind * width
+    mix[2 * block, rows : rows + half, low : low + width] = value[:half].astype(BF16)
+    mix[2 * block + 1, rows : rows + half, low : low + width] = value[half:].astype(BF16)
+
+
+def cell(values):
+    rise = 0.5 * (1.0 + lax.erf(values * (0.5**0.5)))
+    return rise, jnp.exp(-0.5 * values * values) * ((2.0 * math.pi) ** -0.5)
+
+
+def glu_forward_kernel(hidden, table, mix, *refs):
+    pieces = refs[:10]
+    result, normed_out, middle_out, branch_out, glu_out, down_out = refs[10:16]
+    left, right, parts, sems = refs[16:]
+    copies = piece_copies(pieces, sems, glu_spots(left, right))
+    start_all(copies)
+    rows, width = hidden.shape
+    block = width // BLOCKS
+    unit, unused = normalised(hidden[...])
+    normed = (unit * table[1:2] + table[3:4]).astype(BF16)
+    normed_out[...] = normed
+    wait_all(copies)
+    for u in range(2):
+        for b in range(BLOCKS):
+            part = dot(columns(normed, b, block), right[u, b * block : (b + 1) * block]).astype(BF16)
+            for q in range(BLOCKS):
+                middle_out[u, q, :, b * block : (b + 1) * block] = columns(part, q, block)
+    for q in range(BLOCKS):
+        upper = dot(middle_out[0, q], left[0, q])
+        gate = dot(middle_out[1, q], left[1, q])
+        branch_out[0, q] = upper.astype(BF16)
+        branch_out[1, q] = gate.astype(BF16)
+        glu = (gate * cell(gate)[0] * upper).astype(BF16)
+        glu_out[q] = glu
+        parts[q] = dot(glu, down_factor(mix, 7 * block // 6, q))
+    down = [part.astype(BF16) for part in shuffled([parts[q] for q in range(BLOCKS)])]
+    for b in range(BLOCKS):
+        down_out[b] = down[b]
+        span = slice(b * block, (b + 1) * block)
+        result[:, span] = hidden[:, span] + dot(down[b], factor(mix, block // 2, 2, b))
+
+
+def glu_backward_kernel(grad, hidden, table, mix, normed, middle, branch, glu, down, *refs):
+    pieces = refs[:10]
+    result, norm_out, mix_grad, glu_grad = refs[10:14]
+    left, right, low, back, sems, out_sems = refs[14:]
+    copies = piece_copies(pieces, sems, glu_spots(left, right))
+    start_all(copies)
+    rows, width = hidden.shape
+    block = width // BLOCKS
+    incoming = grad[...]
+    half = incoming.astype(BF16)
+    backs = []
+    for b in range(BLOCKS):
+        part = columns(half, b, block)
+        mix_grad[1, b] = dot_rows(down[b], part).astype(BF16)
+        backs.append(dot_columns(part, factor(mix, block // 2, 2, b)))
+    backs = shuffled(backs)
+    for q in range(BLOCKS):
+        low[q] = backs[q].astype(BF16)
+    wait_all(copies)
+    for q in range(BLOCKS):
+        step = low[q]
+        product = dot_rows(glu[q], step).astype(BF16)
+        for index in range(BLOCKS):
+            mix_grad[2 + index, q] = product[index * block : (index + 1) * block]
+        grad_glu = dot_columns(step, down_factor(mix, 7 * block // 6, q))
+        upper = branch[0, q].astype(F32)
+        gate = branch[1, q].astype(F32)
+        rise, density = cell(gate)
+        terms = (grad_glu * gate * rise, grad_glu * upper * (rise + gate * density))
+        for u in range(2):
+            term = terms[u].astype(BF16)
+            wide = dot_columns(term, left[u, q]).astype(BF16)
+            left[u, q] = dot_rows(middle[u, q], term).astype(BF16)
+            for b in range(BLOCKS):
+                back[u, b, :, q * block : (q + 1) * block] = columns(wide, b, block)
+    outgoing = []
+    for b in range(BLOCKS):
+        span = slice(b * block, (b + 1) * block)
+        total = None
+        for u in range(2):
+            term = dot_columns(back[u, b], right[u, span])
+            right[u, span] = dot_rows(normed[:, span], back[u, b]).astype(BF16)
+            total = term if total is None else total + term
+        outgoing.append(total)
+    writes = grad_copies(glu_grad, out_sems, glu_spots(left, right))
+    start_all(writes)
+    through, gain, bias = norm_backward(
+        jnp.concatenate(outgoing, axis=1), hidden[...], table[1:2]
+    )
+    result[...] = incoming + through
+    norm_out[0:1] = gain
+    norm_out[1:2] = bias
+    wait_all(writes)
+
+
+def shifted(values, by):
+    length = values.shape[0]
+    rolled = pltpu.roll(values, by % length, 0)
+    row = lax.broadcasted_iota(jnp.int32, values.shape, 0)
+    keep = row >= by if by > 0 else row < length + by
+    return jnp.where(keep, rolled, 0.0)
+
+
+def two_parts(values):
+    high = values.astype(BF16)
+    return high, (values - high.astype(F32)).astype(BF16)
+
+
+def to_spectrum(waves, values):
+    high, low = two_parts(values)
+    return dot(waves[0], high) + (dot(waves[1], high) + dot(waves[0], low))
+
+
+def from_spectrum(waves, values):
+    high, low = two_parts(values)
+    return dot_rows(waves[0], high) + (dot_rows(waves[1], high) + dot_rows(waves[0], low))
+
+
+def multiplied(spectrum, kernel, back):
+    length = kernel.shape[1]
+    real, imaginary = spectrum[:length], spectrum[length:]
+    sign = -1.0 if back else 1.0
+    return jnp.concatenate(
+        [
+            real * kernel[0] - sign * imaginary * kernel[1],
+            sign * real * kernel[1] + imaginary * kernel[2],
+        ],
+        axis=0,
+    )
+
+
+def mixer_forward_kernel(first_layer, *refs):
+    hidden_in, marked, live, waves, features = refs[:5]
+    pieces = refs[5:15]
+    outs = refs[15:27]
+    (
+        result,
+        hidden_out,
+        mix,
+        table,
+        spectrum_out,
+        kernel_out,
+        filter_out,
+        normed_out,
+        middle_out,
+        saved_out,
+        mixed_out,
+        middle_two_out,
+    ) = outs
+    sems = refs[27]
+    copies = piece_copies(pieces, sems, mix_spots(mix))
+    start_all(copies)
+    wait_all(copies)
+    rows, width = hidden_in.shape
+    block = width // BLOCKS
+    half = block // 2
+    length = waves.shape[2]
+    wide = mix.shape[0]
+    third = 2 * half
+    fourth = third + length - half
+    span = half
+    for w in range(wide):
+        table[:, w * span : (w + 1) * span] = mix[w, third : third + 16, block : block + span].astype(F32)
+    order = length
+    step = order // wide
+    smalls = jnp.concatenate(
+        [mix[w, third + 16 : third + 32, 2 * block : 2 * block + step] for w in range(wide)], axis=1
+    ).astype(F32)
+    middle_filter = jnp.concatenate(
+        [mix[w, third : third + 16, 2 * block : 2 * block + order] for w in range(wide)], axis=0
+    ).astype(F32)
+    last = jnp.concatenate(
+        [
+            mix[w, half:fourth, 3 * block :]
+            for w in range(wide)
+        ],
+        axis=1,
+    ).astype(F32)
+    lead = exact(features[...], smalls[:8]) + smalls[8:9]
+    one = jnp.sin(lead)
+    lead_two = exact(one, middle_filter) + smalls[9:10]
+    two = jnp.sin(lead_two)
+    filter_out[0] = one
+    filter_out[1] = two
+    filter_out[2] = jnp.cos(lead)
+    filter_out[3] = jnp.cos(lead_two)
+    fraction = features[:, 0:1]
+    window = jnp.exp(-fraction * table[8:9])
+    ahead = exact(two, last[:, :width]) * window
+    behind = exact(two, last[:, width:]) * window
+    kernel_out[:, :width] = ahead
+    kernel_out[:, width:] = behind
+    wave = waves[0].astype(F32) + waves[1].astype(F32)
+    row = lax.broadcasted_iota(jnp.int32, (length, 1), 0)
+    weight = jnp.where(row == 0, 0.5 / length, 1.0 / length)
+    sums = exact(wave, ahead + behind)
+    differences = exact(wave[length:], ahead - behind)
+    real = sums[:length]
+    spectrum_out[0] = real * weight
+    spectrum_out[1] = jnp.where(row == 0, 0.0, differences) * weight
+    spectrum_out[2] = jnp.where(row == 0, sums[length : length + 1], real) * weight
+
+    if first_layer:
+        hidden = jnp.where(marked[...] > 0.5, table[9:10], hidden_in[...].astype(F32))
+    else:
+        hidden = hidden_in[...]
+    hidden_out[...] = hidden
+    unit, unused = normalised(hidden)
+    normed = (unit * table[0:1] + table[2:3]).astype(BF16)
+    normed_out[...] = normed
+    for u in range(2):
+        middle, blocks = monarch_small(
+            normed, lambda b: factor(mix, 0, u, b), lambda b: factor(mix, 0, 2 + u, b)
+        )
+        for b in range(BLOCKS):
+            middle_out[u, b] = middle[b]
+        path = jnp.concatenate(blocks, axis=1)
+        saved_out[u] = (path * live[...] if u == 0 else path).astype(BF16)
+        if u == 0:
+            value = path * live[...]
+    gate = path
+    for s in range(rows // length):
+        inside = slice(s * length, (s + 1) * length)
+        alive = live[inside]
+        signal = value[inside]
+        signal = alive * (
+            table[4:5] * shifted(signal, 2) + table[5:6] * shifted(signal, 1) + table[6:7] * signal
+        )
+        product = multiplied(to_spectrum(waves, signal), spectrum_out, False)
+        mixed = from_spectrum(waves, product) + table[7:8] * signal
+        saved_out[2, inside] = mixed.astype(BF16)
+        mixed_out[inside] = (mixed * gate[inside]).astype(BF16)
+    middle, blocks = monarch_small(
+        mixed_out[...], lambda b: factor(mix, half, 0, b), lambda b: factor(mix, half, 1, b)
+    )
+    for b in range(BLOCKS):
+        middle_two_out[b] = middle[b]
+    result[...] = hidden + jnp.concatenate(blocks, axis=1)
+
+
+def mixer_backward_kernel(first_layer, *refs):
+    (
+        grad,
+        hidden_in,
+        marked,
+        live,
+        waves,
+        features,
+        mix,
+        table,
+        spectrum,
+        kernel_in,
+        filters,
+        normed,
+        middle,
+        saved,
+        mixed,
+        middle_two,
+        norm_two,
+        down_grads,
+    ) = refs[:18]
+    result, grad_out = refs[18:20]
+    mix_grad, sum_scratch, value_scratch, table_grad, sems = refs[20:]
+    rows, width = hidden_in.shape
+    block = width // BLOCKS
+    half = block // 2
+    length = waves.shape[2]
+    wide = mix.shape[0]
+    third = 2 * half
+    fourth = third + length - half
+    mix_grad[:, third:fourth] = jnp.zeros((wide, fourth - third, width), BF16)
+    incoming = grad[...]
+    low = incoming.astype(BF16)
+    blocks = [columns(low, b, block) for b in range(BLOCKS)]
+    outs, right_grads, left_grads = monarch_small_backward(
+        mixed[...],
+        [middle_two[b] for b in range(BLOCKS)],
+        blocks,
+        lambda b: factor(mix, half, 0, b),
+        lambda b: factor(mix, half, 1, b),
+    )
+    for b in range(BLOCKS):
+        store_factor(mix_grad, half, 0, b, right_grads[b])
+        store_factor(mix_grad, half, 1, b, left_grads[b])
+        store_factor(mix_grad, half, 2, b, down_grads[1, b])
+        for index in range(4):
+            w = 2 * b + index // 2
+            for part in range(2):
+                position = (index % 2) * 2 + part
+                mix_grad[w, fourth : fourth + half, position * block : (position + 1) * block] = (
+                    down_grads[2 + index, b, part * half : (part + 1) * half]
+                )
+    grad_mixed = jnp.concatenate(outs, axis=1)
+    gate = saved[1].astype(F32)
+    value_scratch[1] = grad_mixed * saved[2].astype(F32)
+    grad_mixed = grad_mixed * gate
+    table_grad[...] = jnp.zeros_like(table_grad)
+    sum_scratch[...] = jnp.zeros_like(sum_scratch)
+    for s in range(rows // length):
+        inside = slice(s * length, (s + 1) * length)
+        alive = live[inside]
+        value = saved[0, inside].astype(F32)
+        behind_two, behind_one = shifted(value, 2), shifted(value, 1)
+        signal = alive * (
+            table[4:5] * behind_two + table[5:6] * behind_one + table[6:7] * value
+        )
+        inner = grad_mixed[inside]
+        table_grad[7:8] += jnp.sum(inner * signal, axis=0, keepdims=True)
+        wave_signal = to_spectrum(waves, signal)
+        wave_grad = to_spectrum(waves, inner)
+        real, imaginary = wave_signal[:length], wave_signal[length:]
+        grad_real, grad_imaginary = wave_grad[:length], wave_grad[length:]
+        sum_scratch[0] += grad_real * real
+        sum_scratch[1] += grad_imaginary * real - grad_real * imaginary
+        sum_scratch[2] += grad_imaginary * imaginary
+        grad_signal = from_spectrum(waves, multiplied(wave_grad, spectrum, True))
+        grad_signal = alive * (grad_signal + table[7:8] * inner)
+        table_grad[4:5] += jnp.sum(grad_signal * behind_two, axis=0, keepdims=True)
+        table_grad[5:6] += jnp.sum(grad_signal * behind_one, axis=0, keepdims=True)
+        table_grad[6:7] += jnp.sum(grad_signal * value, axis=0, keepdims=True)
+        value_scratch[0, inside] = alive * (
+            table[6:7] * grad_signal
+            + table[5:6] * shifted(grad_signal, -1)
+            + table[4:5] * shifted(grad_signal, -2)
+        )
+    row = lax.broadcasted_iota(jnp.int32, (length, 1), 0)
+    weight = jnp.where(row == 0, 0.5 / length, 1.0 / length)
+    wave = waves[0].astype(F32) + waves[1].astype(F32)
+    real = sum_scratch[0] * weight
+    other = sum_scratch[2] * weight
+    turning = jnp.where(row == 0, 0.0, sum_scratch[1] * weight)
+    total = jnp.where(row == 0, real, real + other)
+    last_row = jnp.where(row == 0, other, 0.0)
+    sums = exact(wave[:length], total, (0, 0)) + exact(wave[length:], last_row, (0, 0))
+    differences = exact(wave[length:], turning, (0, 0))
+    fraction = features[:, 0:1]
+    window = jnp.exp(-fraction * table[8:9])
+    count = float(rows // length)
+    grad_ahead = (sums + differences + count * kernel_in[:, :width]) * window
+    grad_behind = (sums - differences + count * kernel_in[:, width:]) * window
+    one, two = filters[0], filters[1]
+    middle_filter = jnp.concatenate(
+        [mix[w, third : third + 16, 2 * block : 2 * block + length] for w in range(wide)], axis=0
+    ).astype(F32)
+    grad_two = None
+    for w in range(wide):
+        source = grad_ahead if w < wide // 2 else grad_behind
+        piece = columns(source, w % (wide // 2), block)
+        factor_out = mix[w, half:fourth, 3 * block :].astype(F32)
+        term = exact(piece, factor_out, (1, 1))
+        grad_two = term if grad_two is None else grad_two + term
+        mix_grad[w, half:fourth, 3 * block :] = exact(two, piece, (0, 0)).astype(BF16)
+    grad_two = grad_two * filters[3]
+    grad_one = exact(grad_two, middle_filter, (1, 1)) * filters[2]
+    filter_grad = exact(one, grad_two, (0, 0)).astype(BF16)
+    smalls = jnp.concatenate(
+        [
+            exact(features[...], grad_one, (0, 0)),
+            jnp.sum(grad_one, axis=0, keepdims=True),
+            jnp.sum(grad_two, axis=0, keepdims=True),
+            jnp.zeros((6, length), F32),
+        ],
+        axis=0,
+    )
+    step = length // wide
+    for w in range(wide):
+        mix_grad[w, third : third + 16, 2 * block : 2 * block + length] = filter_grad[
+            w * step : (w + 1) * step
+        ]
+        mix_grad[w, third + 16 : third + 32, 2 * block : 2 * block + step] = columns(
+            smalls, w, step
+        ).astype(BF16)
+    total_in = None
+    for u in range(2):
+        low = value_scratch[u].astype(BF16)
+        outs, right_grads, left_grads = monarch_small_backward(
+            normed[...],
+            [middle[u, b] for b in range(BLOCKS)],
+            [columns(low, b, block) for b in range(BLOCKS)],
+            lambda b: factor(mix, 0, u, b),
+            lambda b: factor(mix, 0, 2 + u, b),
+        )
+        for b in range(BLOCKS):
+            store_factor(mix_grad, 0, u, b, right_grads[b])
+            store_factor(mix_grad, 0, 2 + u, b, left_grads[b])
+        joint = jnp.concatenate(outs, axis=1)
+        total_in = joint if total_in is None else total_in + joint
+    through, gain, bias = norm_backward(total_in, hidden_in[...], table[0:1])
+    outgoing = incoming + through
+    table_grad[0:1] = gain
+    table_grad[1:2] = norm_two[0:1]
+    table_grad[2:3] = bias
+    table_grad[3:4] = norm_two[1:2]
+    if first_layer:
+        chosen = marked[...] > 0.5
+        table_grad[9:10] = jnp.sum(jnp.where(chosen, outgoing, 0.0), axis=0, keepdims=True)
+        outgoing = jnp.where(chosen, 0.0, outgoing)
+    result[...] = outgoing
+    for w in range(wide):
+        mix_grad[w, third : third + 16, block : block + half] = columns(
+            table_grad[...], w, half
+        ).astype(BF16)
+    writes = grad_copies(grad_out, sems, mix_spots(mix_grad))
+    start_all(writes)
+    wait_all(writes)
+
+
+def call(kernel, name, outs, operands, anywhere, any_outs, scratch):
+    vmem = pl.BlockSpec(memory_space=pltpu.VMEM)
+    any_space = pl.BlockSpec(memory_space=pl.ANY)
+    return pl.pallas_call(
+        kernel,
+        out_shape=[jax.ShapeDtypeStruct(shape, dtype) for shape, dtype in outs],
+        in_specs=[any_space if index in anywhere else vmem for index in range(len(operands))],
+        out_specs=[any_space if index in any_outs else vmem for index in range(len(outs))],
+        scratch_shapes=scratch,
+        compiler_params=pltpu.CompilerParams(vmem_limit_bytes=VMEM_BYTES),
+        name=name,
+    )(*operands)
+
+
+def mixer_forward(first_layer, hidden, marked, live, waves, features, pieces):
+    rows, width = hidden.shape
+    length = waves.shape[2]
+    block = width // BLOCKS
+    quarter = pieces[0].shape[1]
+    outs = [
+        ((rows, width), F32),
+        ((rows, width), F32),
+        ((8, 4 * quarter, width), BF16),
+        ((16, width), F32),
+        ((3, length, width), F32),
+        ((length, 2 * width), F32),
+        ((4, length, length), F32),
+        ((rows, width), BF16),
+        ((2, BLOCKS, rows, block), BF16),
+        ((3, rows, width), BF16),
+        ((rows, width), BF16),
+        ((BLOCKS, rows, block), BF16),
+    ]
+    operands = (hidden, marked, live, waves, features) + tuple(pieces)
+    return call(
+        partial(mixer_forward_kernel, first_layer),
+        "mixer_forward",
+        outs,
+        operands,
+        range(5, 15),
+        (),
+        [pltpu.SemaphoreType.DMA((32,))],
+    )
+
+
+def glu_forward(hidden, table, mix, pieces):
+    rows, width = hidden.shape
+    block = width // BLOCKS
+    outs = [
+        ((rows, width), F32),
+        ((rows, width), BF16),
+        ((2, BLOCKS, rows, width), BF16),
+        ((2, BLOCKS, rows, width), BF16),
+        ((BLOCKS, rows, width), BF16),
+        ((BLOCKS, rows, block), BF16),
+    ]
+    return call(
+        glu_forward_kernel,
+        "glu_forward",
+        outs,
+        (hidden, table, mix) + tuple(pieces),
+        range(3, 13),
+        (),
+        [
+            pltpu.VMEM((2, BLOCKS, width, width), BF16),
+            pltpu.VMEM((2, width, width), BF16),
+            pltpu.VMEM((BLOCKS, rows, block), F32),
+            pltpu.SemaphoreType.DMA((64,)),
+        ],
+    )
+
+
+def glu_backward(grad, hidden, table, mix, saved, pieces):
+    rows, width = hidden.shape
+    block = width // BLOCKS
+    quarter = pieces[0].shape[1]
+    outs = [
+        ((rows, width), F32),
+        ((8, width), F32),
+        ((6, BLOCKS, block, block), BF16),
+        ((2, 2, 2, 4, quarter, width), BF16),
+    ]
+    return call(
+        glu_backward_kernel,
+        "glu_backward",
+        outs,
+        (grad, hidden, table, mix) + tuple(saved) + tuple(pieces),
+        range(9, 19),
+        (3,),
+        [
+            pltpu.VMEM((2, BLOCKS, width, width), BF16),
+            pltpu.VMEM((2, width, width), BF16),
+            pltpu.VMEM((BLOCKS, rows, block), BF16),
+            pltpu.VMEM((2, BLOCKS, rows, width), BF16),
+            pltpu.SemaphoreType.DMA((64,)),
+            pltpu.SemaphoreType.DMA((64,)),
+        ],
+    )
+
+
+def mixer_backward(first_layer, grad, marked, live, waves, features, saved, norm_two, down_grads):
+    hidden, mix, table, spectrum, kernel, filters = saved[:6]
+    rows, width = hidden.shape
+    length = waves.shape[2]
+    outs = [((rows, width), F32), ((2, 2, 2, 4, mix.shape[1] // 4, width), BF16)]
+    operands = (
+        (grad, hidden, marked, live, waves, features)
+        + tuple(saved[1:])
+        + (norm_two, down_grads)
+    )
+    return call(
+        partial(mixer_backward_kernel, first_layer),
+        "mixer_backward",
+        outs,
+        operands,
+        (),
+        (1,),
+        [
+            pltpu.VMEM(mix.shape, BF16),
+            pltpu.VMEM((3, length, width), F32),
+            pltpu.VMEM((2, rows, width), F32),
+            pltpu.VMEM((16, width), F32),
+            pltpu.SemaphoreType.DMA((32,)),
+        ],
+    )
+def neighbour(values, mesh_shape, flip_wide, flip_narrow):
+    wide, narrow = mesh_shape
+    pairs = [
+        (w * narrow + n, (w ^ flip_wide) * narrow + (n ^ flip_narrow))
+        for w in range(wide)
+        for n in range(narrow)
+    ]
+    return lax.ppermute(values, ("wide", "narrow"), pairs)
+
+
+def gather_pieces(part, mesh_shape):
+    own = part[None]
+    own = jnp.concatenate([own, neighbour(own, mesh_shape, 2, 0)], axis=0)
+    own = jnp.concatenate([own, neighbour(own, mesh_shape, 4, 0)], axis=0)
+    along_x = neighbour(own, mesh_shape, 1, 0)
+    along_y = neighbour(own, mesh_shape, 0, 2)
+    low = neighbour(along_y[:2], mesh_shape, 1, 0)
+    high = neighbour(along_x[2:], mesh_shape, 0, 2)
+    near = (own, along_x, along_y, low, high)
+    return near + tuple(neighbour(piece, mesh_shape, 0, 1) for piece in near)
+
+
+def scatter_sum(parts, mesh_shape):
+    def total(own, other):
+        return (own.astype(F32) + other.astype(F32)).astype(BF16)
+
+    both = total(parts[0], neighbour(parts[1], mesh_shape, 0, 1))
+    low, high = both[:, :, :2], both[:, :, 2:]
+    low = total(low[0], neighbour(low[1], mesh_shape, 1, 0))
+    high = total(high[:, 0], neighbour(high[:, 1], mesh_shape, 0, 2))
+    low = total(low[0], neighbour(low[1], mesh_shape, 0, 2))
+    high = total(high[0], neighbour(high[1], mesh_shape, 1, 0))
+    line = total(low, neighbour(high, mesh_shape, 4, 0))
+    return total(line[0], neighbour(line[1], mesh_shape, 2, 0))
+
+
+def ordered(bit, own, other):
+    return jnp.where(bit == 0, jnp.stack([own, other]), jnp.stack([other, own]))
+
+
+def spread(quarter, mesh_shape):
+    unused, unused, y, c = place()
+    pair = ordered(c, quarter, neighbour(quarter, mesh_shape, 0, 1))
+    return ordered(y, pair, neighbour(pair, mesh_shape, 0, 2)).astype(F32)
+
+
+def mix_pack(local, mask_vector):
+    (
+        norm_gain,
+        norm_bias,
+        in_right,
+        in_left,
+        conv_taps,
+        skip_bias,
+        filter_in,
+        filter_in_bias,
+        filter_mid,
+        filter_mid_bias,
+        filter_out,
+        decay_rates,
+        out_right,
+        out_left,
+        unused_right,
+        unused_left,
+        down_right,
+        down_left,
+    ) = local
+    rows, block = in_right.shape[1:]
+    step, order = filter_mid.shape
+    features = filter_in.shape[0]
+    zeros = lambda height, width: jnp.zeros((height, width), BF16)
+    last = [] if mask_vector is None else [mask_vector[None]]
+    table = jnp.concatenate(
+        [norm_gain, norm_bias, conv_taps, skip_bias[None], decay_rates[None]] + last, axis=0
+    )
+    table = jnp.pad(table, ((0, 16 - table.shape[0]), (0, 0)))
+    smalls = jnp.concatenate(
+        [filter_in, zeros(8 - features, step), filter_in_bias[None], filter_mid_bias[None], zeros(6, step)],
+        axis=0,
+    )
+    tail = filter_out[rows:]
+    down = down_right.reshape(4, rows, block)
+    return jnp.concatenate(
+        [
+            jnp.concatenate([in_right[0], in_right[1], in_left[0], in_left[1]], axis=1),
+            jnp.concatenate([out_right, out_left, down_left, filter_out[:rows]], axis=1),
+            jnp.concatenate(
+                [
+                    zeros(16, block),
+                    table,
+                    zeros(16, block - rows),
+                    filter_mid,
+                    zeros(16, block - order),
+                    tail[:16],
+                ],
+                axis=1,
+            ),
+            jnp.concatenate(
+                [zeros(16, 2 * block), smalls, zeros(16, block - step), tail[16:]], axis=1
+            ),
+            jnp.concatenate([down[0], down[1], down[2], down[3]], axis=1),
+        ],
+        axis=0,
+    )
+
+
+def mix_unpack(pack, shards):
+    rows, block = shards[2].shape[2:]
+    order = shards[10].shape[1]
+    step = shards[9].shape[1]
+    features = shards[6].shape[1]
+    third, fourth = 2 * rows, rows + order
+    cut = lambda low, high, k: pack[low:high, k * block : (k + 1) * block]
+    table = pack[third : third + 16, block : block + rows]
+    smalls = pack[third + 16 : third + 32, 2 * block : 2 * block + step]
+    result = {
+        0: table[0:2],
+        1: table[2:4],
+        2: jnp.stack([cut(0, rows, 0), cut(0, rows, 1)]),
+        3: jnp.stack([cut(0, rows, 2), cut(0, rows, 3)]),
+        4: table[4:7],
+        5: table[7],
+        6: smalls[:features],
+        7: smalls[8],
+        8: pack[third : third + step, 2 * block : 2 * block + order],
+        9: smalls[9],
+        10: cut(rows, fourth, 3),
+        12: cut(rows, third, 0),
+        13: cut(rows, third, 1),
+        16: jnp.concatenate([cut(fourth, fourth + rows, k) for k in range(4)], axis=0),
+        17: cut(rows, third, 2),
+    }
+    return result, table[9]
+
+
+def layer_quarters(local, mask_vector):
+    unused, unused, y, c = place()
+    mix = mix_pack(local, mask_vector)
+    rows = mix.shape[0] // 4
+    glu = []
+    for array in (local[15], local[14]):
+        size = array.shape[1] // 2
+        picked = lax.dynamic_index_in_dim(array, y, 0, keepdims=False)
+        glu.append(lax.dynamic_slice_in_dim(picked, c * size, size, 0))
     return (
-        lax.all_gather(shards[0][layer_index], "wide", axis=1, tiled=True),
-        lax.all_gather(shards[1][layer_index], "wide", axis=1, tiled=True),
-        lax.all_gather(shards[2][layer_index], "wide", axis=1, tiled=True),
-        lax.all_gather(shards[3][layer_index], "wide", axis=1, tiled=True),
-        lax.all_gather(shards[4][layer_index], "wide", axis=1, tiled=True),
-        lax.all_gather(shards[5][layer_index], "wide", axis=0, tiled=True),
-        lax.all_gather(shards[6][layer_index], "wide", axis=1, tiled=True),
-        lax.all_gather(shards[7][layer_index], "wide", axis=0, tiled=True),
-        lax.all_gather(shards[8][layer_index], "wide", axis=0, tiled=True),
-        lax.all_gather(shards[9][layer_index], "wide", axis=0, tiled=True),
-        lax.all_gather(shards[10][layer_index], "wide", axis=1, tiled=True),
-        lax.all_gather(shards[11][layer_index], "wide", axis=0, tiled=True),
-        lax.all_gather(shards[12][layer_index], "wide", axis=0, tiled=True),
-        lax.all_gather(shards[13][layer_index], "wide", axis=0, tiled=True),
-        lax.all_gather(shards[14][layer_index], "wide", axis=1, tiled=True),
-        lax.all_gather(shards[15][layer_index], "wide", axis=1, tiled=True),
-        lax.all_gather(shards[16][layer_index], "wide", axis=0, tiled=True),
-        lax.all_gather(shards[17][layer_index], "wide", axis=0, tiled=True),
-    )
-
-
-def scatter_upper(grads):
+        lax.dynamic_slice_in_dim(mix, (2 * y + c) * rows, rows, 0),
+        jnp.concatenate(glu, axis=0),
+    )
+
+
+GRADS = (0, 1, 2, 3, 4, 5, 6, 7, 8, 9, 10, 12, 13, 14, 15, 16, 17)
+SHARD_AXIS = (1, 1, 1, 1, 1, 0, 1, 0, 0, 0, 1, 0, 0, 0, 1, 1, 0, 0)
+
+
+def gather_plain(shards, layer_index):
+    return tuple(
+        lax.all_gather(shards[index][layer_index], "wide", axis=SHARD_AXIS[index], tiled=True)
+        for index in range(18)
+    )
+
+
+def scatter_plain(grads, mask_term):
+    terms = list(grads) + ([] if mask_term is None else [mask_term])
+    axes = [SHARD_AXIS[index] for index in GRADS] + [0]
+    return narrow_total(
+        [
+            lax.psum_scatter(term, "wide", scatter_dimension=axis, tiled=True)
+            for term, axis in zip(terms, axes)
+        ]
+    )
+
+
+def wave_table(length):
+    frequency = np.arange(length)[:, None]
+    places = np.arange(length)[None, :]
+    angles = (frequency * places % (2 * length)) * (math.pi / length)
+    turned = -np.sin(angles)
+    turned[0] = np.where(np.arange(length) % 2 == 0, 1.0, -1.0)
+    table = jnp.asarray(np.concatenate([np.cos(angles), turned]), F32)
+    high = table.astype(BF16)
+    return jnp.stack([high, (table - high.astype(F32)).astype(BF16)])
+
+
+def staged_body(shards, mask_vector, hidden_in, cotangent, live, marked, mesh_shape):
+    rows = hidden_in.shape[0]
+    length = live.shape[1]
+    live = live.reshape(rows, 1)
+    marked = marked.astype(F32)
+    waves = wave_table(length)
+    features = jnp.pad(position_features(length), ((0, 0), (0, 8 - EMB)))
+    pieces = []
+    for layer_index in range(LAYERS):
+        local = tuple(member[layer_index] for member in shards)
+        quarters = layer_quarters(local, mask_vector if layer_index == 0 else None)
+        pieces.append([gather_pieces(quarter, mesh_shape) for quarter in quarters])
+    hidden = hidden_in
+    kept = []
+    for layer_index in range(LAYERS):
+        mixed = mixer_forward(
+            layer_index == 0, hidden, marked, live, waves, features, pieces[layer_index][0]
+        )
+        second = glu_forward(mixed[0], mixed[3], mixed[2], pieces[layer_index][1])
+        kept.append((mixed, second))
+        hidden = second[0]
+    output = hidden.astype(BF16)
+    grad = cotangent.astype(F32)
+    layer_grads = [None] * LAYERS
+    mask_grad = None
+    for layer_index in reversed(range(LAYERS)):
+        mixed, second = kept[layer_index]
+        grad, norm_two, down_grads, glu_grads = glu_backward(
+            grad, mixed[0], mixed[3], mixed[2], second[1:], pieces[layer_index][1]
+        )
+        glu = spread(scatter_sum(glu_grads, mesh_shape), mesh_shape)
+        grad, mix_grads = mixer_backward(
+            layer_index == 0,
+            grad,
+            marked,
+            live,
+            waves,
+            features,
+            mixed[1:],
+            norm_two,
+            down_grads,
+        )
+        mix = spread(scatter_sum(mix_grads, mesh_shape), mesh_shape)
+        found, mask_grad = mix_unpack(mix.reshape(-1, mix.shape[-1]), shards)
+        tall = shards[15].shape[2] // 2
+        found[15] = glu[:, :, :tall].reshape(2, 2 * tall, -1)
+        found[14] = glu[:, :, tall:].reshape(2, shards[14].shape[2], -1)
+        layer_grads[layer_index] = [found[index] for index in GRADS]
+    return output, grad, mask_grad, layer_grads
+
+
+def is_staged(shards, mesh_shape):
+    short, block = shards[2].shape[2:]
+    order, outs = shards[10].shape[1:]
     return (
-        lax.psum_scatter(grads[0], "wide", scatter_dimension=1, tiled=True),
-        lax.psum_scatter(grads[1], "wide", scatter_dimension=1, tiled=True),
-        lax.psum_scatter(grads[2], "wide", scatter_dimension=1, tiled=True),
-        lax.psum_scatter(grads[3], "wide", scatter_dimension=1, tiled=True),
-        lax.psum_scatter(grads[4], "wide", scatter_dimension=1, tiled=True),
-        lax.psum_scatter(grads[5], "wide", scatter_dimension=0, tiled=True),
-        lax.psum_scatter(grads[6], "wide", scatter_dimension=1, tiled=True),
-        lax.psum_scatter(grads[7], "wide", scatter_dimension=0, tiled=True),
-        lax.psum_scatter(grads[8], "wide", scatter_dimension=0, tiled=True),
-        lax.psum_scatter(grads[9], "wide", scatter_dimension=0, tiled=True),
-        lax.psum_scatter(grads[10], "wide", scatter_dimension=1, tiled=True),
-        lax.psum_scatter(grads[11], "wide", scatter_dimension=0, tiled=True),
-        lax.psum_scatter(grads[12], "wide", scatter_dimension=0, tiled=True),
-        lax.psum_scatter(grads[13], "wide", scatter_dimension=1, tiled=True),
-        lax.psum_scatter(grads[14], "wide", scatter_dimension=1, tiled=True),
-        lax.psum_scatter(grads[15], "wide", scatter_dimension=0, tiled=True),
-        lax.psum_scatter(grads[16], "wide", scatter_dimension=0, tiled=True),
-    )
-
-
-def scatter_lower(grads, mask_term):
-    return (
-        lax.psum_scatter(grads[0], "wide", scatter_dimension=1, tiled=True),
-        lax.psum_scatter(grads[1], "wide", scatter_dimension=1, tiled=True),
-        lax.psum_scatter(grads[2], "wide", scatter_dimension=1, tiled=True),
-        lax.psum_scatter(grads[3], "wide", scatter_dimension=1, tiled=True),
-        lax.psum_scatter(grads[4], "wide", scatter_dimension=1, tiled=True),
-        lax.psum_scatter(grads[5], "wide", scatter_dimension=0, tiled=True),
-        lax.psum_scatter(grads[6], "wide", scatter_dimension=1, tiled=True),
-        lax.psum_scatter(grads[7], "wide", scatter_dimension=0, tiled=True),
-        lax.psum_scatter(grads[8], "wide", scatter_dimension=0, tiled=True),
-        lax.psum_scatter(grads[9], "wide", scatter_dimension=0, tiled=True),
-        lax.psum_scatter(grads[10], "wide", scatter_dimension=1, tiled=True),
-        lax.psum_scatter(grads[11], "wide", scatter_dimension=0, tiled=True),
-        lax.psum_scatter(grads[12], "wide", scatter_dimension=0, tiled=True),
-        lax.psum_scatter(grads[13], "wide", scatter_dimension=1, tiled=True),
-        lax.psum_scatter(grads[14], "wide", scatter_dimension=1, tiled=True),
-        lax.psum_scatter(grads[15], "wide", scatter_dimension=0, tiled=True),
-        lax.psum_scatter(grads[16], "wide", scatter_dimension=0, tiled=True),
-        lax.psum_scatter(mask_term, "wide", scatter_dimension=0, tiled=True),
+        tuple(mesh_shape) == (8, 4)
+        and short == 96
+        and block == 192
+        and order == 128
+        and outs == block
+        and shards[14].shape[2:] == (short, 8 * short)
+        and shards[15].shape[2:] == (4 * short, 8 * short)
     )
 
 
@@ -435,7 +1321,39 @@
     return result
 
 
+def plain_body(shards, mask_vector, hidden_in, cotangent, live_mask, marked):
+    seq_count = live_mask.shape[0]
+    mask_full = lax.all_gather(mask_vector, "wide", axis=0, tiled=True)
+    weights = [gather_plain(shards, layer_index) for layer_index in range(LAYERS)]
+    hidden = jnp.where(
+        marked, mask_full.astype(jnp.float32)[None, :], hidden_in.astype(jnp.float32)
+    )
+    saved_layers = []
+    for layer_index in range(LAYERS):
+        hidden, saved = forward_layer(hidden, weights[layer_index], live_mask)
+        saved_layers.append(saved)
+    output = hidden.astype(jnp.bfloat16)
+    share = 0.5 * seq_count
+    grad_hidden = cotangent.astype(jnp.float32)
+    layer_grads = [None] * LAYERS
+    mask_grad = None
+    for layer_index in reversed(range(LAYERS)):
+        grad_hidden, grads = backward_layer(
+            grad_hidden, weights[layer_index], saved_layers[layer_index], live_mask, share
+        )
+        if layer_index > 0:
+            layer_grads[layer_index] = scatter_plain(grads, None)
+        else:
+            mask_term = jnp.sum(jnp.where(marked, grad_hidden, 0.0), axis=0)
+            reduced = scatter_plain(grads, mask_term)
+            layer_grads[0] = reduced[:-1]
+            mask_grad = reduced[-1]
+    grad_input = jnp.where(marked, 0.0, grad_hidden)
+    return output, grad_input, mask_grad, layer_grads
+
+
 def body(
+    mesh_shape,
     hidden_in,
     seq_lengths,
     mask_positions,
@@ -468,36 +1386,6 @@
     marked = jnp.any(mask_positions[:, :, None] == places[None, None, :], axis=1).reshape(
         row_count, 1
     )
-    gathered = (
-        lax.all_gather(mask_vector, "wide", axis=0, tiled=True),
-        lax.all_gather(norm_gain, "wide", axis=2, tiled=True),
-        lax.all_gather(norm_bias, "wide", axis=2, tiled=True),
-        lax.all_gather(in_right, "wide", axis=2, tiled=True),
-        lax.all_gather(in_left, "wide", axis=2, tiled=True),
-        lax.all_gather(conv_taps, "wide", axis=2, tiled=True),
-        lax.all_gather(skip_bias, "wide", axis=1, tiled=True),
-        lax.all_gather(filter_in, "wide", axis=2, tiled=True),
-        lax.all_gather(filter_in_bias, "wide", axis=1, tiled=True),
-        lax.all_gather(filter_mid, "wide", axis=1, tiled=True),
-        lax.all_gather(filter_mid_bias, "wide", axis=1, tiled=True),
-        lax.all_gather(filter_out, "wide", axis=2, tiled=True),
-        lax.all_gather(decay_rates, "wide", axis=1, tiled=True),
-        lax.all_gather(out_right, "wide", axis=1, tiled=True),
-        lax.all_gather(out_left, "wide", axis=1, tiled=True),
-        lax.all_gather(glu_right, "wide", axis=2, tiled=True),
-        lax.all_gather(glu_left, "wide", axis=2, tiled=True),
-        lax.all_gather(down_right, "wide", axis=1, tiled=True),
-        lax.all_gather(down_left, "wide", axis=1, tiled=True),
-    )
-    hidden = jnp.where(
-        marked, gathered[0].astype(jnp.float32)[None, :], hidden_in.astype(jnp.float32)
-    )
-    saved_layers = []
-    for layer_index in range(LAYERS):
-        layer_weights = tuple((member[layer_index] for member in gathered[1:]))
-        hidden, saved = forward_layer(hidden, layer_weights, live_mask)
-        saved_layers.append(saved)
-    output = hidden.astype(jnp.bfloat16)
     shards = (
         norm_gain,
         norm_bias,
@@ -518,27 +1406,18 @@
         down_right,
         down_left,
     )
-    share = 0.5 * seq_count
-    grad_hidden = cotangent.astype(jnp.float32)
-    layer_grads = [None] * LAYERS
-    mask_grad = None
-    for layer_index in reversed(range(LAYERS)):
-        layer_weights = fetch_layer(shards, layer_index)
-        grad_hidden, grads = backward_layer(
-            grad_hidden, layer_weights, saved_layers[layer_index], live_mask, share
+    if is_staged(shards, mesh_shape):
+        output, grad_input, mask_grad, layer_grads = staged_body(
+            shards, mask_vector, hidden_in, cotangent, live_mask, marked, mesh_shape
         )
-        if layer_index > 0:
-            layer_grads[layer_index] = narrow_total(scatter_upper(grads))
-        else:
-            mask_term = jnp.sum(jnp.where(marked, grad_hidden, 0.0), axis=0)
-            reduced = narrow_total(scatter_lower(grads, mask_term))
-            layer_grads[0] = reduced[:-1]
-            mask_grad = reduced[-1]
+    else:
+        output, grad_input, mask_grad, layer_grads = plain_body(
+            shards, mask_vector, hidden_in, cotangent, live_mask, marked
+        )
     final_grads = [
         jnp.stack([layer_grads[position][member_index] for position in range(LAYERS)])
         for member_index in range(17)
     ]
-    grad_input = jnp.where(marked, 0.0, grad_hidden)
     return (output, grad_input, mask_grad) + tuple(final_grads)
 
 
@@ -569,7 +1448,7 @@
         P(None, "wide", None),
     )
     return jax.shard_map(
-        body,
+        partial(body, (mesh.shape["wide"], mesh.shape["narrow"])),
         mesh=mesh,
         in_specs=placed,
         out_specs=(

time: 4410 us -> 742 us (0.17)
  waiting for transfers between devices: 2310 us -> 388 us
  blocking collectives: 1200 us -> 0 us
  local copies, waits for them, and re-layouts: 477 us -> 50.8 us
  matrix products: 278 us -> 0 us
  Pallas kernels: 0 us -> 173 us
  starting transfers between devices: 2.26 us -> 70.9 us
  other arithmetic: 108 us -> 48.1 us
    reduce_scatter x20 -> x0, waiting for transfers between devices: 1860 us -> none  [the longest x1 315 us: scatter_lower(): lax.psum_scatter(grads[14], 'wide', scatter_dimension=1, tiled=True)]
    all_gather x33 -> x0, blocking collectives: 1130 us -> none  [the longest x2 99.7 us: fetch_layer(): lax.all_gather(shards[17][layer_index], 'wide', axis=0, tiled=True)]
    ppermute x0 -> x80, waiting for transfers between devices: none -> 388 us  [neighbour(): return lax.ppermute(values, ('wide', 'narrow'), pairs)]
    unnamed x48 -> x0, waiting for transfers between devices: 375 us -> none
    dot_general x128 -> x0, matrix products: 276 us -> none  [the longest x12 45.5 us: monarch_forward(): jnp.einsum('rbi,bio->rbo', middle, left_blocks, preferred_element_type=jn...]
    pallas_call x0 -> x8, Pallas kernels: none -> 173 us  [call(): pl.pallas_call(kernel, out_shape=[jax.ShapeDtypeStruct(shape, dtype) for...]
    slice x61 -> x28, local copies, waits for them, and re-layouts: 140 us -> 9.03 us  [the longest x6 2.47 us: staged_body(): local = tuple((member[layer_index] for member in shards))]
    psum x1 -> x0, waiting for transfers between devices: 76.5 us -> none  [narrow_total(): lax.psum(flattened.astype(jnp.bfloat16), 'narrow').astype(jnp.float32)]
  transfers between devices with their start and end apart: 40 -> 80, of which waited for: 27 -> 40; matrix products, arithmetic and copies ran while one was open for 8% -> 9% of each run, Pallas kernels for 0% -> 14%
where the time goes in v1:
time: 742 us; the launch traced here: 733 us
  waiting for transfers between devices  388 us (52%)
  Pallas kernels  173 us (23%)
  starting transfers between devices  70.9 us (10%)
  local copies, waits for them, and re-layouts  50.8 us (7%)
  other arithmetic  48.1 us (6%)
    ppermute x80, waiting for transfers between devices, neighbour(): return lax.ppermute(values, ('wide', 'narrow'), pairs)  388 us
    pallas_call x8, Pallas kernels, call(): pl.pallas_call(kernel, out_shape=[jax.ShapeDtypeStruct(shape, dtype) for...  173 us
    ppermute x80, starting transfers between devices, neighbour(): return lax.ppermute(values, ('wide', 'narrow'), pairs)  70.9 us
    convert_element_type x20, other arithmetic, total(): return (own.astype(F32) + other.astype(F32)).astype(BF16)  19.8 us
    unnamed x150, local copies, waits for them, and re-layouts  15.3 us
  transfers between devices with their start and end apart: 80, of which 40 were waited for; matrix products, arithmetic and copies ran while one was open for 9% of the time, Pallas kernels for 14%

profile of v1, /device:TPU:0, one launch (start us, length us, event | category | flops | bytes accessed | tf_op | source)
XLA Modules:
  0.0 733.0 jit_solution(15929903491826526676)
XLA Ops:
  35.0 14.3 %collective-permute-done.1 = bf16[2,80,768]{2,1,0:T(8,128)(2,1)S(1)} collective-permute-done((bf16[2,80,768]{2,1,0:T(8,128)(2,1)S(1)}, bf16[2,80,768]{2,1,0:T(8,128)(2,1)S(1)}, u32[]{:S(2)}, u32[]{:S(2)}) %collective-permute-start.1) | collective-permute-done | bytes 245792 | tf_op jit(solution)/shard_map/ppermute | solution.py:1072
  67.9 38.2 %collective-permute-done.12 = bf16[2,240,768]{2,1,0:T(8,128)(2,1)S(1)} collective-permute-done((bf16[2,240,768]{2,1,0:T(8,128)(2,1)S(1)}, bf16[2,240,768]{2,1,0:T(8,128)(2,1)S(1)}, u32[]{:S(2)}, u32[]{:S(2)}) %collective-permute-start.12) | collective-permute-done | bytes 737312 | tf_op jit(solution)/shard_map/ppermute | solution.py:1072
  109.8 6.7 collective-permute-done.34
  118.8 21.5 %collective-permute-done.27.refs_9_ = bf16[2,80,768]{2,1,0:T(8,128)(2,1)S(1)} collective-permute-done((bf16[2,80,768]{2,1,0:T(8,128)(2,1)S(1)}, bf16[2,80,768]{2,1,0:T(8,128)(2,1)S(1)}, u32[]{:S(2)}, u32[]{:S(2)}) %collective-permute-start.27) | collective-permute-done | bytes 245792 | tf_op jit(solution)/shard_map/ppermute | solution.py:1072
  151.4 24.2 %collective-permute-done.13.refs_1_ = bf16[4,240,768]{2,1,0:T(8,128)(2,1)S(1)} collective-permute-done((bf16[4,240,768]{2,1,0:T(8,128)(2,1)S(1)}, bf16[4,240,768]{2,1,0:T(8,128)(2,1)S(1)}, u32[]{:S(2)}, u32[]{:S(2)}) %collective-permute-start.13) | collective-permute-done | bytes 1474592 | tf_op jit(solution)/shard_map/ppermute | solution.py:1072
  179.6 27.7 %collective-permute-done.35.refs_1_ = bf16[4,240,768]{2,1,0:T(8,128)(2,1)} collective-permute-done((bf16[4,240,768]{2,1,0:T(8,128)(2,1)S(1)}, bf16[4,240,768]{2,1,0:T(8,128)(2,1)}, u32[]{:S(2)}, u32[]{:S(2)}) %collective-permute-start.35) | collective-permute-done | bytes 1474592 | tf_op jit(solution)/shard_map/ppermute | solution.py:1072
  210.0 13.0 %collective-permute-done.15.refs_3_ = bf16[2,240,768]{2,1,0:T(8,128)(2,1)S(1)} collective-permute-done((bf16[2,240,768]{2,1,0:T(8,128)(2,1)S(1)}, bf16[2,240,768]{2,1,0:T(8,128)(2,1)S(1)}, u32[]{:S(2)}, u32[]{:S(2)}) %collective-permute-start.15) | collective-permute-done | bytes 737312 | tf_op jit(solution)/shard_map/ppermute | solution.py:1072
  224.5 14.0 %collective-permute-done.37.refs_3_ = bf16[2,240,768]{2,1,0:T(8,128)(2,1)} collective-permute-done((bf16[2,240,768]{2,1,0:T(8,128)(2,1)S(1)}, bf16[2,240,768]{2,1,0:T(8,128)(2,1)}, u32[]{:S(2)}, u32[]{:S(2)}) %collective-permute-start.37) | collective-permute-done | bytes 737312 | tf_op jit(solution)/shard_map/ppermute | solution.py:1072
  250.4 14.9 %mixer_forward.2 = (f32[384,768]{1,0:T(8,128)}, f32[384,768]{1,0:T(8,128)}, bf16[8,320,768]{2,1,0:T(8,128)(2,1)}, f32[16,768]{1,0:T(8,128)}, f32[3,128,768]{2,1,...) custom-call(bf16[384,768]{1,0:T(8,128)(2,1)} %refs_0_.1, ...), custom_call_target="tpu_custom_call" | custom-call | tf_op jit(solution)/shard_map/mixer_forward/pallas_call | solution.py:943
  265.3 16.9 %glu_forward.2 = (f32[384,768]{1,0:T(8,128)}, bf16[384,768]{1,0:T(8,128)(2,1)}, bf16[2,4,384,768]{3,2,1,0:T(8,128)(2,1)}, bf16[2,4,384,768]{3,2,1,0:T(8,128)(2,1...) custom-call(f32[384,768]{1,0:T(8,128)} %get-tuple-element.68.hidden, ...), custom_call_target="tpu_custom_call" | custom-call | tf_op jit(solution)/shard_map/glu_forward/pallas_call | solution.py:943
  282.2 14.7 %mixer_forward.3 = (f32[384,768]{1,0:T(8,128)}, f32[384,768]{1,0:T(8,128)}, bf16[8,320,768]{2,1,0:T(8,128)(2,1)}, f32[16,768]{1,0:T(8,128)}, f32[3,128,768]{2,1,...) custom-call(f32[384,768]{1,0:T(8,128)} %get-tuple-element.71.refs_0_, ...), custom_call_target="tpu_custom_call" | custom-call | tf_op jit(solution)/shard_map/mixer_forward/pallas_call | solution.py:943
  298.0 16.8 %glu_forward.3 = (f32[384,768]{1,0:T(8,128)}, bf16[384,768]{1,0:T(8,128)(2,1)}, bf16[2,4,384,768]{3,2,1,0:T(8,128)(2,1)}, bf16[2,4,384,768]{3,2,1,0:T(8,128)(2,1...) custom-call(f32[384,768]{1,0:T(8,128)} %get-tuple-element.72.hidden, ...), custom_call_target="tpu_custom_call" | custom-call | tf_op jit(solution)/shard_map/glu_forward/pallas_call | solution.py:943
  314.8 33.5 %glu_backward.2 = (f32[384,768]{1,0:T(8,128)}, f32[8,768]{1,0:T(8,128)}, bf16[6,4,192,192]{3,2,1,0:T(8,128)(2,1)}, bf16[2,2,2,4,240,768]{5,4,3,2,1,0:T(8,128)(2,1)}) custom-call(f32[384,768]{1,0:T(8,128)} %convert_element_type.391.grad, f32[384,768]{1,0:T(8,128)} %get-tuple-element.72.hidden, f32[16,768]{1,0:T(8,128)} %get-tuple-element.73.table.refs_7_, ...), custom_call_target="tpu_custom_call" | custom-call | tf_op jit(solution)/shard_map/glu_backward/pallas_call | solution.py:943
  348.3 21.1 %mixer_backward.2 = (f32[384,768]{1,0:T(8,128)}, bf16[2,2,2,4,80,768]{5,4,3,2,1,0:T(8,128)(2,1)}) custom-call(f32[384,768]{1,0:T(8,128)} %get-tuple-element.81.refs_0_, f32[384,768]{1,0:T(8,128)} %get-tuple-element.82.refs_1_, f32[384,1]{1,0:T(8,128)} %bitcast.373, f32[384,1]{1,0:T(8,128)} %bitcast.369, bf16[2,256,128]{2,1,0:T(8,128)(2,1)} %constant.196.refs_3_.refs_4_, ...), custom_call_target="tpu_custom_call" | custom-call | tf_op jit(solution)/shard_map/mixer_backward/pallas_call | solution.py:943
  372.9 33.2 %glu_backward.3 = (f32[384,768]{1,0:T(8,128)}, f32[8,768]{1,0:T(8,128)}, bf16[6,4,192,192]{3,2,1,0:T(8,128)(2,1)}, bf16[2,2,2,4,240,768]{5,4,3,2,1,0:T(8,128)(2,1)}) custom-call(f32[384,768]{1,0:T(8,128)} %get-tuple-element.93.grad, f32[384,768]{1,0:T(8,128)} %get-tuple-element.68.hidden, f32[16,768]{1,0:T(8,128)} %get-tuple-element.69.table.refs_7_, ...), custom_call_target="tpu_custom_call" | custom-call | tf_op jit(solution)/shard_map/glu_backward/pallas_call | solution.py:943
  406.1 21.7 %mixer_backward.3 = (f32[384,768]{1,0:T(8,128)}, bf16[2,2,2,4,80,768]{5,4,3,2,1,0:T(8,128)(2,1)}) custom-call(f32[384,768]{1,0:T(8,128)} %get-tuple-element.99.refs_0_, f32[384,768]{1,0:T(8,128)} %get-tuple-element.100.refs_1_, f32[384,1]{1,0:T(8,128)} %bitcast.374, f32[384,1]{1,0:T(8,128)} %bitcast.370, bf16[2,256,128]{2,1,0:T(8,128)(2,1)} %constant.196.refs_3_.refs_4_, ...), custom_call_target="tpu_custom_call" | custom-call | tf_op jit(solution)/shard_map/mixer_backward/pallas_call | solution.py:943
  442.8 6.4 collective-permute-done.54
  453.4 6.4 collective-permute-done.45
  473.6 9.3 %collective-permute-start.59 = (bf16[80,768]{1,0:T(8,128)(2,1)S(1)}, bf16[80,768]{1,0:T(8,128)(2,1)S(1)}, u32[]{:S(2)}, u32[]{:S(2)}) collective-permute-start(bf16[80,768]{1,0:T(8,128)(2,1)S(1)} %slice_bitcast_fusion.44), channel_id=1, source_target_pairs={{0,8},{1,9},{2,10},{3,11},{4,12},{5,13},{6,14},{7,15},{8,0},{9,1},... | collective-permute-start | bytes 368648 | tf_op jit(solution)/shard_map/ppermute | solution.py:1072
  482.9 6.2 collective-permute-done.49
  500.8 6.6 collective-permute-done.61
  519.2 6.0 fusion
  538.6 23.4 %collective-permute-done.72 = bf16[2,2,240,768]{3,2,1,0:T(8,128)(2,1)} collective-permute-done((bf16[2,2,240,768]{3,2,1,0:T(8,128)(2,1)}, bf16[2,2,240,768]{3,2,1,0:T(8,128)(2,1)}, u32[]{:S(2)}, u32[]{:S(2)}) %collective-permute-start.72) | collective-permute-done | bytes 1474592 | tf_op jit(solution)/shard_map/ppermute | solution.py:1072
  568.4 25.1 %collective-permute-done.63 = bf16[2,2,240,768]{3,2,1,0:T(8,128)(2,1)S(1)} collective-permute-done((bf16[2,2,240,768]{3,2,1,0:T(8,128)(2,1)S(1)}, bf16[2,2,240,768]{3,2,1,0:T(8,128)(2,1)S(1)}, u32[]{:S(2)}, u32[]{:S(2)}) %collective-permute-start.63) | collective-permute-done | bytes 1474592 | tf_op jit(solution)/shard_map/ppermute | solution.py:1072
  597.9 11.4 %collective-permute-done.75 = bf16[2,240,768]{2,1,0:T(8,128)(2,1)S(1)} collective-permute-done((bf16[2,240,768]{2,1,0:T(8,128)(2,1)S(1)}, bf16[2,240,768]{2,1,0:T(8,128)(2,1)S(1)}, u32[]{:S(2)}, u32[]{:S(2)}) %collective-permute-start.75) | collective-permute-done | bytes 737312 | tf_op jit(solution)/shard_map/ppermute | solution.py:1072
  611.6 11.7 %collective-permute-done.66 = bf16[2,240,768]{2,1,0:T(8,128)(2,1)S(1)} collective-permute-done((bf16[2,240,768]{2,1,0:T(8,128)(2,1)S(1)}, bf16[2,240,768]{2,1,0:T(8,128)(2,1)S(1)}, u32[]{:S(2)}, u32[]{:S(2)}) %collective-permute-start.66) | collective-permute-done | bytes 737312 | tf_op jit(solution)/shard_map/ppermute | solution.py:1072
  624.0 32.4 %collective-permute-done.76 = bf16[2,240,768]{2,1,0:T(8,128)(2,1)S(1)} collective-permute-done((bf16[2,240,768]{2,1,0:T(8,128)(2,1)S(1)}, bf16[2,240,768]{2,1,0:T(8,128)(2,1)S(1)}, u32[]{:S(2)}, u32[]{:S(2)}) %collective-permute-start.76) | collective-permute-done | bytes 737312 | tf_op jit(solution)/shard_map/ppermute | solution.py:1072
  656.9 15.4 %collective-permute-done.67 = bf16[2,240,768]{2,1,0:T(8,128)(2,1)S(1)} collective-permute-done((bf16[2,240,768]{2,1,0:T(8,128)(2,1)S(1)}, bf16[2,240,768]{2,1,0:T(8,128)(2,1)S(1)}, u32[]{:S(2)}, u32[]{:S(2)}) %collective-permute-start.67) | collective-permute-done | bytes 737312 | tf_op jit(solution)/shard_map/ppermute | solution.py:1072
  672.7 7.5 %collective-permute-done.77 = bf16[240,768]{1,0:T(8,128)(2,1)S(1)} collective-permute-done((bf16[240,768]{1,0:T(8,128)(2,1)S(1)}, bf16[240,768]{1,0:T(8,128)(2,1)S(1)}, u32[]{:S(2)}, u32[]{:S(2)}) %collective-permute-start.77) | collective-permute-done | bytes 368672 | tf_op jit(solution)/shard_map/ppermute | solution.py:1072
  680.3 7.6 %collective-permute-done.68 = bf16[240,768]{1,0:T(8,128)(2,1)S(1)} collective-permute-done((bf16[240,768]{1,0:T(8,128)(2,1)S(1)}, bf16[240,768]{1,0:T(8,128)(2,1)S(1)}, u32[]{:S(2)}, u32[]{:S(2)}) %collective-permute-start.68) | collective-permute-done | bytes 368672 | tf_op jit(solution)/shard_map/ppermute | solution.py:1072
  698.2 11.2 %collective-permute-done.79 = bf16[2,240,768]{2,1,0:T(8,128)(2,1)} collective-permute-done((bf16[2,240,768]{2,1,0:T(8,128)(2,1)}, bf16[2,240,768]{2,1,0:T(8,128)(2,1)}, u32[]{:S(2)}, u32[]{:S(2)}) %collective-permute-start.79) | collective-permute-done | bytes 737312 | tf_op jit(solution)/shard_map/ppermute | solution.py:1072
  712.6 12.1 %collective-permute-done.70 = bf16[2,240,768]{2,1,0:T(8,128)(2,1)} collective-permute-done((bf16[2,240,768]{2,1,0:T(8,128)(2,1)}, bf16[2,240,768]{2,1,0:T(8,128)(2,1)}, u32[]{:S(2)}, u32[]{:S(2)}) %collective-permute-start.70) | collective-permute-done | bytes 737312 | tf_op jit(solution)/shard_map/ppermute | solution.py:1072
  (464 shorter events, 199.5 us)
Async XLA Ops:
  25.7 31.4 %collective-permute-start.11 = (bf16[1,240,768]{2,1,0:T(8,128)(2,1)S(1)}, bf16[1,240,768]{2,1,0:T(8,128)(2,1)S(1)}, u32[]{:S(2)}, u32[]{:S(2)}) collective-permute-start(bf16[1,240,768]{2,1,0:T(8,128)(2,1)S(1)} %maximum_bitcast_fusion.2), channel_id=1, source_target_pairs={{0,8},{1,9},{2,10},{3,11},{4,12},{5,13},{6,14},{7,15},{8,0},{9,1},... | collective-permute-start | bytes 1105928 | tf_op jit(solution)/shard_map/ppermute | solution.py:1072
  57.3 48.8 %collective-permute-start.12 = (bf16[2,240,768]{2,1,0:T(8,128)(2,1)S(1)}, bf16[2,240,768]{2,1,0:T(8,128)(2,1)S(1)}, u32[]{:S(2)}, u32[]{:S(2)}) collective-permute-start(bf16[2,240,768]{2,1,0:T(8,128)(2,1)S(1)} %pad_maximum_fusion.5), channel_id=1, source_target_pairs={{0,16},{1,17},{2,18},{3,19},{4,20},{5,21},{6,22},{7,23},{8,24},{9,... | collective-permute-start | bytes 2211848 | tf_op jit(solution)/shard_map/ppermute | solution.py:1072
  61.7 54.8 %collective-permute-start.34 = (bf16[2,240,768]{2,1,0:T(8,128)(2,1)S(1)}, bf16[2,240,768]{2,1,0:T(8,128)(2,1)S(1)}, u32[]{:S(2)}, u32[]{:S(2)}) collective-permute-start(bf16[2,240,768]{2,1,0:T(8,128)(2,1)S(1)} %pad_maximum_fusion.6), channel_id=1, source_target_pairs={{0,16},{1,17},{2,18},{3,19},{4,20},{5,21},{6,22},{7,23},{8,24},{9,... | collective-permute-start | bytes 2211848 | tf_op jit(solution)/shard_map/ppermute | solution.py:1072
  62.0 45.8 %collective-permute-start.28 = (bf16[4,80,768]{2,1,0:T(8,128)(2,1)S(1)}, bf16[4,80,768]{2,1,0:T(8,128)(2,1)S(1)}, u32[]{:S(2)}, u32[]{:S(2)}) collective-permute-start(bf16[4,80,768]{2,1,0:T(8,128)(2,1)S(1)} %pad_maximum_fusion.8.refs_5_), channel_id=1, source_target_pairs={{0,1},{1,0},{2,3},{3,2},{4,5},{5,4},{6,7},{7,6},{8,9},{9,8},{10,11... | collective-permute-start | bytes 1474568 | tf_op jit(solution)/shard_map/ppermute | solution.py:1072
  65.7 42.6 %collective-permute-start.24 = (bf16[4,80,768]{2,1,0:T(8,128)(2,1)S(1)}, bf16[4,80,768]{2,1,0:T(8,128)(2,1)S(1)}, u32[]{:S(2)}, u32[]{:S(2)}) collective-permute-start(bf16[4,80,768]{2,1,0:T(8,128)(2,1)S(1)} %pad_maximum_fusion.8.refs_5_), channel_id=1, source_target_pairs={{0,4},{1,5},{2,6},{3,7},{4,0},{5,1},{6,2},{7,3},{8,12},{9,13},{10,... | collective-permute-start | bytes 1474568 | tf_op jit(solution)/shard_map/ppermute | solution.py:1072
  66.8 49.8 %collective-permute-start.4 = (bf16[2,80,768]{2,1,0:T(8,128)(2,1)S(1)}, bf16[2,80,768]{2,1,0:T(8,128)(2,1)S(1)}, u32[]{:S(2)}, u32[]{:S(2)}) collective-permute-start(bf16[2,80,768]{2,1,0:T(8,128)(2,1)S(1)} %slice.723), channel_id=1, source_target_pairs={{0,4},{1,5},{2,6},{3,7},{4,0},{5,1},{6,2},{7,3},{8,12},{9,13},{10,... | collective-permute-start | bytes 737288 | tf_op jit(solution)/shard_map/ppermute | solution.py:1072
  107.7 40.1 %collective-permute-start.14 = (bf16[4,240,768]{2,1,0:T(8,128)(2,1)S(1)}, bf16[4,240,768]{2,1,0:T(8,128)(2,1)S(1)}, u32[]{:S(2)}, u32[]{:S(2)}) collective-permute-start(bf16[4,240,768]{2,1,0:T(8,128)(2,1)S(1)} %pad_maximum_fusion.1.refs_0_), channel_id=1, source_target_pairs={{0,2},{1,3},{2,0},{3,1},{4,6},{5,7},{6,4},{7,5},{8,10},{9,11},{10,... | collective-permute-start | bytes 4423688 | tf_op jit(solution)/shard_map/ppermute | solution.py:1072
  140.4 35.1 %collective-permute-start.13 = (bf16[4,240,768]{2,1,0:T(8,128)(2,1)S(1)}, bf16[4,240,768]{2,1,0:T(8,128)(2,1)S(1)}, u32[]{:S(2)}, u32[]{:S(2)}) collective-permute-start(bf16[4,240,768]{2,1,0:T(8,128)(2,1)S(1)} %pad_maximum_fusion.1.refs_0_), channel_id=1, source_target_pairs={{0,4},{1,5},{2,6},{3,7},{4,0},{5,1},{6,2},{7,3},{8,12},{9,13},{10,... | collective-permute-start | bytes 4423688 | tf_op jit(solution)/shard_map/ppermute | solution.py:1072
  142.0 34.5 %collective-permute-start.36 = (bf16[4,240,768]{2,1,0:T(8,128)(2,1)S(1)}, bf16[4,240,768]{2,1,0:T(8,128)(2,1)}, u32[]{:S(2)}, u32[]{:S(2)}) collective-permute-start(bf16[4,240,768]{2,1,0:T(8,128)(2,1)S(1)} %pad_maximum_fusion.2.refs_0_), channel_id=1, source_target_pairs={{0,2},{1,3},{2,0},{3,1},{4,6},{5,7},{6,4},{7,5},{8,10},{9,11},{10,... | collective-permute-start | bytes 4423688 | tf_op jit(solution)/shard_map/ppermute | solution.py:1072
  145.9 32.0 %collective-permute-start.17 = (bf16[4,240,768]{2,1,0:T(8,128)(2,1)S(1)}, bf16[4,240,768]{2,1,0:T(8,128)(2,1)S(1)}, u32[]{:S(2)}, u32[]{:S(2)}) collective-permute-start(bf16[4,240,768]{2,1,0:T(8,128)(2,1)S(1)} %pad_maximum_fusion.1.refs_0_), channel_id=1, source_target_pairs={{0,1},{1,0},{2,3},{3,2},{4,5},{5,4},{6,7},{7,6},{8,9},{9,8},{10,11... | collective-permute-start | bytes 4423688 | tf_op jit(solution)/shard_map/ppermute | solution.py:1072
  147.3 60.0 %collective-permute-start.35 = (bf16[4,240,768]{2,1,0:T(8,128)(2,1)S(1)}, bf16[4,240,768]{2,1,0:T(8,128)(2,1)}, u32[]{:S(2)}, u32[]{:S(2)}) collective-permute-start(bf16[4,240,768]{2,1,0:T(8,128)(2,1)S(1)} %pad_maximum_fusion.2.refs_0_), channel_id=1, source_target_pairs={{0,4},{1,5},{2,6},{3,7},{4,0},{5,1},{6,2},{7,3},{8,12},{9,13},{10,... | collective-permute-start | bytes 4423688 | tf_op jit(solution)/shard_map/ppermute | solution.py:1072
  150.3 72.7 %collective-permute-start.15 = (bf16[2,240,768]{2,1,0:T(8,128)(2,1)S(1)}, bf16[2,240,768]{2,1,0:T(8,128)(2,1)S(1)}, u32[]{:S(2)}, u32[]{:S(2)}) collective-permute-start(bf16[2,240,768]{2,1,0:T(8,128)(2,1)S(1)} %slice.725), channel_id=1, source_target_pairs={{0,4},{1,5},{2,6},{3,7},{4,0},{5,1},{6,2},{7,3},{8,12},{9,13},{10,... | collective-permute-start | bytes 2211848 | tf_op jit(solution)/shard_map/ppermute | solution.py:1072
  175.6 65.2 %collective-permute-start.19 = (bf16[4,240,768]{2,1,0:T(8,128)(2,1)S(1)}, bf16[4,240,768]{2,1,0:T(8,128)(2,1)S(1)}, u32[]{:S(2)}, u32[]{:S(2)}) collective-permute-start(bf16[4,240,768]{2,1,0:T(8,128)(2,1)S(1)} %collective-permute-done.14.refs_2_), channel_id=1, source_target_pairs={{0,1},{1,0},{2,3},{3,2},{4,5},{5,4},{6,7},{7,6},{8,9},{9,8},{10,11... | collective-permute-start | bytes 4423688 | tf_op jit(solution)/shard_map/ppermute | solution.py:1072
  176.5 64.8 %collective-permute-start.18 = (bf16[4,240,768]{2,1,0:T(8,128)(2,1)S(1)}, bf16[4,240,768]{2,1,0:T(8,128)(2,1)S(1)}, u32[]{:S(2)}, u32[]{:S(2)}) collective-permute-start(bf16[4,240,768]{2,1,0:T(8,128)(2,1)S(1)} %collective-permute-done.13.refs_1_), channel_id=1, source_target_pairs={{0,1},{1,0},{2,3},{3,2},{4,5},{5,4},{6,7},{7,6},{8,9},{9,8},{10,11... | collective-permute-start | bytes 4423688 | tf_op jit(solution)/shard_map/ppermute | solution.py:1072
  178.0 46.5 %collective-permute-start.16 = (bf16[2,240,768]{2,1,0:T(8,128)(2,1)S(1)}, bf16[2,240,768]{2,1,0:T(8,128)(2,1)S(1)}, u32[]{:S(2)}, u32[]{:S(2)}) collective-permute-start(bf16[2,240,768]{2,1,0:T(8,128)(2,1)S(1)} %slice.726), channel_id=1, source_target_pairs={{0,2},{1,3},{2,0},{3,1},{4,6},{5,7},{6,4},{7,5},{8,10},{9,11},{10,... | collective-permute-start | bytes 2211848 | tf_op jit(solution)/shard_map/ppermute | solution.py:1072
  240.8 56.0 %collective-permute-start.39 = (bf16[4,240,768]{2,1,0:T(8,128)(2,1)S(1)}, bf16[4,240,768]{2,1,0:T(8,128)(2,1)S(1)}, u32[]{:S(2)}, u32[]{:S(2)}) collective-permute-start(bf16[4,240,768]{2,1,0:T(8,128)(2,1)S(1)} %pad_maximum_fusion.2.refs_0_), channel_id=1, source_target_pairs={{0,1},{1,0},{2,3},{3,2},{4,5},{5,4},{6,7},{7,6},{8,9},{9,8},{10,11... | collective-permute-start | bytes 4423688 | tf_op jit(solution)/shard_map/ppermute | solution.py:1072
  240.8 56.0 %collective-permute-start.41 = (bf16[4,240,768]{2,1,0:T(8,128)(2,1)}, bf16[4,240,768]{2,1,0:T(8,128)(2,1)}, u32[]{:S(2)}, u32[]{:S(2)}) collective-permute-start(bf16[4,240,768]{2,1,0:T(8,128)(2,1)} %collective-permute-done.36.refs_2_), channel_id=1, source_target_pairs={{0,1},{1,0},{2,3},{3,2},{4,5},{5,4},{6,7},{7,6},{8,9},{9,8},{10,11... | collective-permute-start | bytes 4423688 | tf_op jit(solution)/shard_map/ppermute | solution.py:1072
  241.4 55.5 %collective-permute-start.40 = (bf16[4,240,768]{2,1,0:T(8,128)(2,1)}, bf16[4,240,768]{2,1,0:T(8,128)(2,1)}, u32[]{:S(2)}, u32[]{:S(2)}) collective-permute-start(bf16[4,240,768]{2,1,0:T(8,128)(2,1)} %collective-permute-done.35.refs_1_), channel_id=1, source_target_pairs={{0,1},{1,0},{2,3},{3,2},{4,5},{5,4},{6,7},{7,6},{8,9},{9,8},{10,11... | collective-permute-start | bytes 4423688 | tf_op jit(solution)/shard_map/ppermute | solution.py:1072
  242.5 54.4 %collective-permute-start.42 = (bf16[2,240,768]{2,1,0:T(8,128)(2,1)}, bf16[2,240,768]{2,1,0:T(8,128)(2,1)}, u32[]{:S(2)}, u32[]{:S(2)}) collective-permute-start(bf16[2,240,768]{2,1,0:T(8,128)(2,1)} %collective-permute-done.37.refs_3_), channel_id=1, source_target_pairs={{0,1},{1,0},{2,3},{3,2},{4,5},{5,4},{6,7},{7,6},{8,9},{9,8},{10,11... | collective-permute-start | bytes 2211848 | tf_op jit(solution)/shard_map/ppermute | solution.py:1072
  243.4 53.5 %collective-permute-start.43 = (bf16[2,240,768]{2,1,0:T(8,128)(2,1)}, bf16[2,240,768]{2,1,0:T(8,128)(2,1)}, u32[]{:S(2)}, u32[]{:S(2)}) collective-permute-start(bf16[2,240,768]{2,1,0:T(8,128)(2,1)} %collective-permute-done.38.refs_4_), channel_id=1, source_target_pairs={{0,1},{1,0},{2,3},{3,2},{4,5},{5,4},{6,7},{7,6},{8,9},{9,8},{10,11... | collective-permute-start | bytes 2211848 | tf_op jit(solution)/shard_map/ppermute | solution.py:1072
  372.4 62.1 %collective-permute-start.53 = (bf16[2,2,4,80,768]{4,3,2,0,1:T(8,128)(2,1)}, bf16[2,2,4,80,768]{4,3,2,0,1:T(8,128)(2,1)S(1)}, u32[]{:S(2)}, u32[]{:S(2)}) collective-permute-start(bf16[2,2,4,80,768]{4,3,2,0,1:T(8,128)(2,1)} %slice_bitcast_fusion.3), channel_id=1, source_target_pairs={{0,1},{1,0},{2,3},{3,2},{4,5},{5,4},{6,7},{7,6},{8,9},{9,8},{10,11... | collective-permute-start | bytes 5898248 | tf_op jit(solution)/shard_map/ppermute | solution.py:1072
  434.0 85.2 %collective-permute-start.71 = (bf16[2,2,4,240,768]{4,3,2,0,1:T(8,128)(2,1)S(1)}, bf16[2,2,4,240,768]{4,3,2,0,1:T(8,128)(2,1)}, u32[]{:S(2)}, u32[]{:S(2)}) collective-permute-start(bf16[2,2,4,240,768]{4,3,2,0,1:T(8,128)(2,1)S(1)} %slice_bitcast_fusion), channel_id=1, source_target_pairs={{0,1},{1,0},{2,3},{3,2},{4,5},{5,4},{6,7},{7,6},{8,9},{9,8},{10,11... | collective-permute-start | bytes 17694728 | tf_op jit(solution)/shard_map/ppermute | solution.py:1072
  498.1 32.8 %collective-permute-start.62 = (bf16[2,2,4,240,768]{4,3,2,1,0:T(8,128)(2,1)}, bf16[2,2,4,240,768]{4,3,2,1,0:T(8,128)(2,1)}, u32[]{:S(2)}, u32[]{:S(2)}) collective-permute-start(bf16[2,2,4,240,768]{4,3,2,1,0:T(8,128)(2,1)} %slice_bitcast_fusion.2), channel_id=1, source_target_pairs={{0,1},{1,0},{2,3},{3,2},{4,5},{5,4},{6,7},{7,6},{8,9},{9,8},{10,11... | collective-permute-start | bytes 17694728 | tf_op jit(solution)/shard_map/ppermute | solution.py:1072
  526.5 35.5 %collective-permute-start.72 = (bf16[2,2,240,768]{3,2,1,0:T(8,128)(2,1)}, bf16[2,2,240,768]{3,2,1,0:T(8,128)(2,1)}, u32[]{:S(2)}, u32[]{:S(2)}) collective-permute-start(bf16[2,2,240,768]{3,2,1,0:T(8,128)(2,1)} %slice_bitcast_fusion.8), channel_id=1, source_target_pairs={{0,4},{1,5},{2,6},{3,7},{4,0},{5,1},{6,2},{7,3},{8,12},{9,13},{10,... | collective-permute-start | bytes 4423688 | tf_op jit(solution)/shard_map/ppermute | solution.py:1072
  529.2 35.5 %collective-permute-start.74 = (bf16[2,2,240,768]{3,2,1,0:T(8,128)(2,1)}, bf16[2,2,240,768]{3,2,1,0:T(8,128)(2,1)}, u32[]{:S(2)}, u32[]{:S(2)}) collective-permute-start(bf16[2,2,240,768]{3,2,1,0:T(8,128)(2,1)} %slice_bitcast_fusion.6), channel_id=1, source_target_pairs={{0,2},{1,3},{2,0},{3,1},{4,6},{5,7},{6,4},{7,5},{8,10},{9,11},{10,... | collective-permute-start | bytes 4423688 | tf_op jit(solution)/shard_map/ppermute | solution.py:1072
  536.8 56.7 %collective-permute-start.63 = (bf16[2,2,240,768]{3,2,1,0:T(8,128)(2,1)S(1)}, bf16[2,2,240,768]{3,2,1,0:T(8,128)(2,1)S(1)}, u32[]{:S(2)}, u32[]{:S(2)}) collective-permute-start(bf16[2,2,240,768]{3,2,1,0:T(8,128)(2,1)S(1)} %slice_bitcast_fusion.12), channel_id=1, source_target_pairs={{0,4},{1,5},{2,6},{3,7},{4,0},{5,1},{6,2},{7,3},{8,12},{9,13},{10,... | collective-permute-start | bytes 4423688 | tf_op jit(solution)/shard_map/ppermute | solution.py:1072
  537.9 56.2 %collective-permute-start.65 = (bf16[2,2,240,768]{3,2,1,0:T(8,128)(2,1)S(1)}, bf16[2,2,240,768]{3,2,1,0:T(8,128)(2,1)S(1)}, u32[]{:S(2)}, u32[]{:S(2)}) collective-permute-start(bf16[2,2,240,768]{3,2,1,0:T(8,128)(2,1)S(1)} %slice_bitcast_fusion.10), channel_id=1, source_target_pairs={{0,2},{1,3},{2,0},{3,1},{4,6},{5,7},{6,4},{7,5},{8,10},{9,11},{10,... | collective-permute-start | bytes 4423688 | tf_op jit(solution)/shard_map/ppermute | solution.py:1072
  567.4 41.9 %collective-permute-start.75 = (bf16[2,240,768]{2,1,0:T(8,128)(2,1)S(1)}, bf16[2,240,768]{2,1,0:T(8,128)(2,1)S(1)}, u32[]{:S(2)}, u32[]{:S(2)}) collective-permute-start(bf16[2,240,768]{2,1,0:T(8,128)(2,1)S(1)} %slice_bitcast_fusion.14), channel_id=1, source_target_pairs={{0,4},{1,5},{2,6},{3,7},{4,0},{5,1},{6,2},{7,3},{8,12},{9,13},{10,... | collective-permute-start | bytes 2211848 | tf_op jit(solution)/shard_map/ppermute | solution.py:1072
  609.5 46.9 %collective-permute-start.76 = (bf16[2,240,768]{2,1,0:T(8,128)(2,1)S(1)}, bf16[2,240,768]{2,1,0:T(8,128)(2,1)S(1)}, u32[]{:S(2)}, u32[]{:S(2)}) collective-permute-start(bf16[2,240,768]{2,1,0:T(8,128)(2,1)S(1)} %fusion.10), channel_id=1, source_target_pairs={{0,16},{1,17},{2,18},{3,19},{4,20},{5,21},{6,22},{7,23},{8,24},{9,... | collective-permute-start | bytes 2211848 | tf_op jit(solution)/shard_map/ppermute | solution.py:1072
  609.8 47.0 %collective-permute-start.64 = (bf16[2,240,768]{2,1,0:T(8,128)(2,1)S(1)}, bf16[2,240,768]{2,1,0:T(8,128)(2,1)S(1)}, u32[]{:S(2)}, u32[]{:S(2)}) collective-permute-start(bf16[2,240,768]{2,1,0:T(8,128)(2,1)S(1)} %slice_bitcast_fusion.20), channel_id=1, source_target_pairs={{0,2},{1,3},{2,0},{3,1},{4,6},{5,7},{6,4},{7,5},{8,10},{9,11},{10,... | collective-permute-start | bytes 2211848 | tf_op jit(solution)/shard_map/ppermute | solution.py:1072
  623.5 48.8 %collective-permute-start.67 = (bf16[2,240,768]{2,1,0:T(8,128)(2,1)S(1)}, bf16[2,240,768]{2,1,0:T(8,128)(2,1)S(1)}, u32[]{:S(2)}, u32[]{:S(2)}) collective-permute-start(bf16[2,240,768]{2,1,0:T(8,128)(2,1)S(1)} %fusion.12), channel_id=1, source_target_pairs={{0,16},{1,17},{2,18},{3,19},{4,20},{5,21},{6,22},{7,23},{8,24},{9,... | collective-permute-start | bytes 2211848 | tf_op jit(solution)/shard_map/ppermute | solution.py:1072
  692.4 32.4 %collective-permute-start.70 = (bf16[2,240,768]{2,1,0:T(8,128)(2,1)}, bf16[2,240,768]{2,1,0:T(8,128)(2,1)}, u32[]{:S(2)}, u32[]{:S(2)}) collective-permute-start(bf16[2,240,768]{2,1,0:T(8,128)(2,1)} %maximum_select_fusion.3), channel_id=1, source_target_pairs={{0,2},{1,3},{2,0},{3,1},{4,6},{5,7},{6,4},{7,5},{8,10},{9,11},{10,... | collective-permute-start | bytes 2211848 | tf_op jit(solution)/shard_map/ppermute | solution.py:1072
  (114 other events, 2304.1 us)

commit v2 on v1

--- a/solution.py
+++ b/solution.py
@@ -426,9 +426,6 @@
     return w // 2, w % 2, n // 2, n % 2
 
 
-KINDS = ((0, 0, 0, 4), (1, 0, 0, 4), (0, 1, 0, 4), (1, 1, 0, 2), (1, 1, 2, 2))
-
-
 def relative(z, distance):
     high, low = z // 2, z % 2
     return 2 * flip(high, distance // 2) + flip(low, distance % 2)
@@ -438,13 +435,13 @@
     z, x, y, c = place()
     copies = []
     for core in range(2):
-        for kind, (dx, dy, first, count) in enumerate(KINDS):
-            source = pieces[core * len(KINDS) + kind]
-            for slot in range(count):
-                owner = (relative(z, first + slot), flip(x, dx), flip(y, dy), flip(c, core))
-                for row, target in targets_of(*owner):
-                    view = source.at[slot, pl.ds(row, target.shape[0])]
-                    copies.append(pltpu.make_async_copy(view, target, sems.at[len(copies)]))
+        for dx in range(2):
+            for dy in range(2):
+                for dz in range(4):
+                    owner = (relative(z, dz), flip(x, dx), flip(y, dy), flip(c, core))
+                    for row, target in targets_of(*owner):
+                        view = pieces.at[core, dx, dy, dz, pl.ds(row, target.shape[0])]
+                        copies.append(pltpu.make_async_copy(view, target, sems.at[len(copies)]))
     return copies
 
 
@@ -539,9 +536,8 @@
 
 
 def glu_forward_kernel(hidden, table, mix, *refs):
-    pieces = refs[:10]
-    result, normed_out, middle_out, branch_out, glu_out, down_out = refs[10:16]
-    left, right, parts, sems = refs[16:]
+    pieces, result, normed_out, middle_out, branch_out, glu_out, down_out = refs[:7]
+    left, right, parts, sems = refs[7:]
     copies = piece_copies(pieces, sems, glu_spots(left, right))
     start_all(copies)
     rows, width = hidden.shape
@@ -571,9 +567,8 @@
 
 
 def glu_backward_kernel(grad, hidden, table, mix, normed, middle, branch, glu, down, *refs):
-    pieces = refs[:10]
-    result, norm_out, mix_grad, glu_grad = refs[10:14]
-    left, right, low, back, sems, out_sems = refs[14:]
+    pieces, result, norm_out, mix_grad, glu_grad = refs[:5]
+    left, right, low, back, sems, out_sems = refs[5:]
     copies = piece_copies(pieces, sems, glu_spots(left, right))
     start_all(copies)
     rows, width = hidden.shape
@@ -663,8 +658,8 @@
 
 def mixer_forward_kernel(first_layer, *refs):
     hidden_in, marked, live, waves, features = refs[:5]
-    pieces = refs[5:15]
-    outs = refs[15:27]
+    pieces = refs[5]
+    outs = refs[6:18]
     (
         result,
         hidden_out,
@@ -679,7 +674,7 @@
         mixed_out,
         middle_two_out,
     ) = outs
-    sems = refs[27]
+    sems = refs[18]
     copies = piece_copies(pieces, sems, mix_spots(mix))
     start_all(copies)
     wait_all(copies)
@@ -937,6 +932,9 @@
     wait_all(writes)
 
 
+COSTS = {"mixer_forward": 17, "glu_forward": 20, "glu_backward": 38, "mixer_backward": 24}
+
+
 def call(kernel, name, outs, operands, anywhere, any_outs, scratch):
     vmem = pl.BlockSpec(memory_space=pltpu.VMEM)
     any_space = pl.BlockSpec(memory_space=pl.ANY)
@@ -947,6 +945,9 @@
         out_specs=[any_space if index in any_outs else vmem for index in range(len(outs))],
         scratch_shapes=scratch,
         compiler_params=pltpu.CompilerParams(vmem_limit_bytes=VMEM_BYTES),
+        cost_estimate=pl.CostEstimate(
+            flops=COSTS[name] * 10**9, bytes_accessed=COSTS[name] * 10**6, transcendentals=0
+        ),
         name=name,
     )(*operands)
 
@@ -955,7 +956,7 @@
     rows, width = hidden.shape
     length = waves.shape[2]
     block = width // BLOCKS
-    quarter = pieces[0].shape[1]
+    quarter = pieces.shape[4]
     outs = [
         ((rows, width), F32),
         ((rows, width), F32),
@@ -970,13 +971,13 @@
         ((rows, width), BF16),
         ((BLOCKS, rows, block), BF16),
     ]
-    operands = (hidden, marked, live, waves, features) + tuple(pieces)
+    operands = (hidden, marked, live, waves, features, pieces)
     return call(
         partial(mixer_forward_kernel, first_layer),
         "mixer_forward",
         outs,
         operands,
-        range(5, 15),
+        (5,),
         (),
         [pltpu.SemaphoreType.DMA((32,))],
     )
@@ -997,8 +998,8 @@
         glu_forward_kernel,
         "glu_forward",
         outs,
-        (hidden, table, mix) + tuple(pieces),
-        range(3, 13),
+        (hidden, table, mix, pieces),
+        (3,),
         (),
         [
             pltpu.VMEM((2, BLOCKS, width, width), BF16),
@@ -1012,7 +1013,7 @@
 def glu_backward(grad, hidden, table, mix, saved, pieces):
     rows, width = hidden.shape
     block = width // BLOCKS
-    quarter = pieces[0].shape[1]
+    quarter = pieces.shape[4]
     outs = [
         ((rows, width), F32),
         ((8, width), F32),
@@ -1023,8 +1024,8 @@
         glu_backward_kernel,
         "glu_backward",
         outs,
-        (grad, hidden, table, mix) + tuple(saved) + tuple(pieces),
-        range(9, 19),
+        (grad, hidden, table, mix) + tuple(saved) + (pieces,),
+        (9,),
         (3,),
         [
             pltpu.VMEM((2, BLOCKS, width, width), BF16),
@@ -1062,50 +1063,265 @@
             pltpu.SemaphoreType.DMA((32,)),
         ],
     )
-def neighbour(values, mesh_shape, flip_wide, flip_narrow):
-    wide, narrow = mesh_shape
-    pairs = [
-        (w * narrow + n, (w ^ flip_wide) * narrow + (n ^ flip_narrow))
-        for w in range(wide)
-        for n in range(narrow)
+PEERS = ((1, 0, 0, 0), (2, 0, 0, 0), (3, 0, 0, 0), (0, 1, 0, 0), (0, 0, 1, 0), (0, 0, 0, 1))
+ALONG_X, ALONG_Y, ACROSS = PEERS[3], PEERS[4], PEERS[5]
+
+
+def peer(distance, dx, dy, dc):
+    z, x, y, c = place()
+    return (2 * relative(z, distance) + flip(x, dx), 2 * flip(y, dy) + flip(c, dc))
+
+
+def greet():
+    barrier = pltpu.get_barrier_semaphore()
+    for target in PEERS:
+        pl.semaphore_signal(
+            barrier, inc=1, device_id=peer(*target), device_id_type=pl.DeviceIdType.MESH
+        )
+    pl.semaphore_wait(barrier, len(PEERS))
+
+
+class Mail:
+    def __init__(self, sent, received):
+        self.sent, self.received, self.copies = sent, received, []
+
+    def send(self, source, target, to):
+        index = len(self.copies)
+        copy = pltpu.make_async_remote_copy(
+            src_ref=source,
+            dst_ref=target,
+            send_sem=self.sent.at[index],
+            recv_sem=self.received.at[index],
+            device_id=peer(*to),
+            device_id_type=pl.DeviceIdType.MESH,
+        )
+        copy.start()
+        self.copies.append(copy)
+        return copy
+
+    def finish(self):
+        for copy in self.copies:
+            copy.wait_send()
+
+
+GATHER_COPIES = 12
+
+
+def gather_steps(mail, own, pieces, rows):
+    view = lambda core, dx, dy, first, count: pieces.at[core, dx, dy, pl.ds(first, count), rows]
+    along_z = [
+        mail.send(own, pieces.at[0, 0, 0, distance, rows], PEERS[distance - 1])
+        for distance in (1, 2, 3)
     ]
-    return lax.ppermute(values, ("wide", "narrow"), pairs)
-
-
-def gather_pieces(part, mesh_shape):
-    own = part[None]
-    own = jnp.concatenate([own, neighbour(own, mesh_shape, 2, 0)], axis=0)
-    own = jnp.concatenate([own, neighbour(own, mesh_shape, 4, 0)], axis=0)
-    along_x = neighbour(own, mesh_shape, 1, 0)
-    along_y = neighbour(own, mesh_shape, 0, 2)
-    low = neighbour(along_y[:2], mesh_shape, 1, 0)
-    high = neighbour(along_x[2:], mesh_shape, 0, 2)
-    near = (own, along_x, along_y, low, high)
-    return near + tuple(neighbour(piece, mesh_shape, 0, 1) for piece in near)
-
-
-def scatter_sum(parts, mesh_shape):
-    def total(own, other):
-        return (own.astype(F32) + other.astype(F32)).astype(BF16)
-
-    both = total(parts[0], neighbour(parts[1], mesh_shape, 0, 1))
-    low, high = both[:, :, :2], both[:, :, 2:]
-    low = total(low[0], neighbour(low[1], mesh_shape, 1, 0))
-    high = total(high[:, 0], neighbour(high[:, 1], mesh_shape, 0, 2))
-    low = total(low[0], neighbour(low[1], mesh_shape, 0, 2))
-    high = total(high[0], neighbour(high[1], mesh_shape, 1, 0))
-    line = total(low, neighbour(high, mesh_shape, 4, 0))
-    return total(line[0], neighbour(line[1], mesh_shape, 2, 0))
-
-
-def ordered(bit, own, other):
-    return jnp.where(bit == 0, jnp.stack([own, other]), jnp.stack([other, own]))
-
-
-def spread(quarter, mesh_shape):
+    yield
+    for copy in along_z:
+        copy.wait_recv()
+    along_x = mail.send(view(0, 0, 0, 0, 4), view(0, 1, 0, 0, 4), ALONG_X)
+    along_y = mail.send(view(0, 0, 0, 0, 4), view(0, 0, 1, 0, 4), ALONG_Y)
+    across = [mail.send(view(0, 0, 0, 0, 4), view(1, 0, 0, 0, 4), ACROSS)]
+    yield
+    along_y.wait_recv()
+    low = mail.send(view(0, 0, 1, 0, 2), view(0, 1, 1, 0, 2), ALONG_X)
+    across.append(mail.send(view(0, 0, 1, 0, 4), view(1, 0, 1, 0, 4), ACROSS))
+    along_x.wait_recv()
+    high = mail.send(view(0, 1, 0, 2, 2), view(0, 1, 1, 2, 2), ALONG_Y)
+    across.append(mail.send(view(0, 1, 0, 0, 4), view(1, 1, 0, 0, 4), ACROSS))
+    yield
+    low.wait_recv()
+    across.append(mail.send(view(0, 1, 1, 0, 2), view(1, 1, 1, 0, 2), ACROSS))
+    high.wait_recv()
+    across.append(mail.send(view(0, 1, 1, 2, 2), view(1, 1, 1, 2, 2), ACROSS))
+    yield
+    for copy in across:
+        copy.wait_recv()
+    yield
+
+
+def pipeline(starts, ahead):
+    running = []
+    waiting = list(starts)
+    while waiting or running:
+        if waiting:
+            running.append(waiting.pop(0)())
+        for chunk in list(running):
+            try:
+                next(chunk)
+            except StopIteration:
+                running.remove(chunk)
+
+
+def gather_kernel(counts, *refs):
+    groups = len(counts)
+    owns, pieces = refs[:groups], refs[groups : 2 * groups]
+    sent, received, local = refs[2 * groups :]
+    mail = Mail(sent, received)
+    greet()
+    copies = []
+    for index in range(groups):
+        copy = pltpu.make_async_copy(owns[index], pieces[index].at[0, 0, 0, 0], local.at[index])
+        copy.start()
+        copies.append(copy)
+    starts = []
+    for index, count in enumerate(counts):
+        size = owns[index].shape[0] // count
+        for part in range(count):
+            rows = pl.ds(part * size, size)
+            starts.append(
+                partial(gather_steps, mail, owns[index].at[rows], pieces[index], rows)
+            )
+    wait_all(copies)
+    pipeline(starts, 1)
+    mail.finish()
+
+
+def gather_all(quarters, counts, number):
+    anywhere = pl.BlockSpec(memory_space=pl.ANY)
+    total = GATHER_COPIES * sum(counts)
+    return pl.pallas_call(
+        partial(gather_kernel, counts),
+        out_shape=[
+            jax.ShapeDtypeStruct((2, 2, 2, 4) + quarter.shape, quarter.dtype)
+            for quarter in quarters
+        ],
+        in_specs=[anywhere] * len(quarters),
+        out_specs=[anywhere] * len(quarters),
+        scratch_shapes=[
+            pltpu.SemaphoreType.DMA((total,)),
+            pltpu.SemaphoreType.DMA((total,)),
+            pltpu.SemaphoreType.DMA((len(quarters),)),
+        ],
+        compiler_params=pltpu.CompilerParams(collective_id=number, has_side_effects=True),
+        name="gather",
+    )(*quarters)
+
+
+SCATTER_COPIES = 11
+
+
+def scatter_steps(mail, local, grads, rows, result, spots, buffers):
+    first, one, two_x, two_y, three, four, own, last = buffers
+    x_core = mail.send(grads.at[1, :, :, :, rows], one, ACROSS)
+    load = pltpu.make_async_copy(grads.at[0, :, :, :, rows], first, local.at[0])
+    load.start()
+    yield
+    load.wait()
+    x_core.wait_recv()
+    for dx in range(2):
+        for dy in range(2):
+            first[dx, dy] += one[dx, dy]
+    low = mail.send(first.at[1, :, pl.ds(0, 2)], two_x, ALONG_X)
+    high = mail.send(first.at[:, 1, pl.ds(2, 2)], two_y, ALONG_Y)
+    yield
+    low.wait_recv()
+    for dy in (1, 0):
+        two_x[dy] += first[0, dy, 0:2]
+        if dy == 1:
+            low = mail.send(two_x.at[1], three.at[pl.ds(0, 2)], ALONG_Y)
+    high.wait_recv()
+    for dx in (1, 0):
+        two_y[dx] += first[dx, 0, 2:4]
+        if dx == 1:
+            high = mail.send(two_y.at[1], three.at[pl.ds(2, 2)], ALONG_X)
+    yield
+    low.wait_recv()
+    three[0:2] += two_x[0]
+    along_z = [mail.send(three.at[1], four.at[0], PEERS[0])]
+    high.wait_recv()
+    three[2:4] += two_y[0]
+    along_z += [mail.send(three.at[d], four.at[d - 1], PEERS[d - 1]) for d in (2, 3)]
+    yield
+    total = three[0].astype(F32)
+    for index, copy in enumerate(along_z):
+        copy.wait_recv()
+        total = total + four[index].astype(F32)
+    own[...] = total.astype(BF16)
+    mine, theirs = spots
+    across = [mail.send(own, result.at[mine, rows], ACROSS)]
+    along_y = mail.send(own, last, ALONG_Y)
+    keep = pltpu.make_async_copy(own, result.at[mine, rows], local.at[1])
+    keep.start()
+    yield
+    along_y.wait_recv()
+    across.append(mail.send(last, result.at[theirs, rows], ACROSS))
+    keep_too = pltpu.make_async_copy(last, result.at[theirs, rows], local.at[2])
+    keep_too.start()
+    yield
+    for copy in across:
+        copy.wait_recv()
+    keep.wait()
+    keep_too.wait()
+    yield
+
+
+def scatter_buffers(size, width):
+    return [
+        pltpu.VMEM((2, 2, 4, size, width), BF16),
+        pltpu.VMEM((2, 2, 4, size, width), BF16),
+        pltpu.VMEM((2, 2, size, width), BF16),
+        pltpu.VMEM((2, 2, size, width), BF16),
+        pltpu.VMEM((4, size, width), BF16),
+        pltpu.VMEM((3, size, width), BF16),
+        pltpu.VMEM((size, width), BF16),
+        pltpu.VMEM((size, width), BF16),
+    ]
+
+
+def scatter_kernel(counts, *refs):
+    groups = len(counts)
+    chunks = sum(counts)
+    grads, results = refs[:groups], refs[groups : 2 * groups]
+    sent, received, local = refs[2 * groups : 2 * groups + 3]
+    buffers = refs[2 * groups + 3 :]
+    mail = Mail(sent, received)
     unused, unused, y, c = place()
-    pair = ordered(c, quarter, neighbour(quarter, mesh_shape, 0, 1))
-    return ordered(y, pair, neighbour(pair, mesh_shape, 0, 2)).astype(F32)
+    spots = (2 * y + c, 2 * (1 - y) + c)
+    greet()
+    starts = []
+    for index, count in enumerate(counts):
+        size = results[index].shape[1] // count
+        for part in range(count):
+            number = len(starts)
+            starts.append(
+                partial(
+                    scatter_steps,
+                    mail,
+                    local.at[number],
+                    grads[index],
+                    pl.ds(part * size, size),
+                    results[index],
+                    spots,
+                    buffers[8 * number : 8 * number + 8],
+                )
+            )
+    pipeline(starts, 1)
+    mail.finish()
+
+
+def scatter_all(grads, counts, number):
+    anywhere = pl.BlockSpec(memory_space=pl.ANY)
+    chunks = sum(counts)
+    size, width = grads[0].shape[4] // counts[0], grads[0].shape[5]
+    buffers = []
+    for index, count in enumerate(counts):
+        for part in range(count):
+            buffers += scatter_buffers(grads[index].shape[4] // count, width)
+    total = SCATTER_COPIES * chunks
+    return pl.pallas_call(
+        partial(scatter_kernel, counts),
+        out_shape=[jax.ShapeDtypeStruct((4,) + array.shape[4:], BF16) for array in grads],
+        in_specs=[anywhere] * len(grads),
+        out_specs=[anywhere] * len(grads),
+        scratch_shapes=[
+            pltpu.SemaphoreType.DMA((total,)),
+            pltpu.SemaphoreType.DMA((total,)),
+            pltpu.SemaphoreType.DMA((chunks, 3)),
+        ]
+        + buffers,
+        compiler_params=pltpu.CompilerParams(
+            collective_id=number, has_side_effects=True, vmem_limit_bytes=VMEM_BYTES
+        ),
+        name="scatter",
+    )(*grads)
 
 
 def mix_pack(local, mask_vector):
@@ -1252,30 +1468,29 @@
     marked = marked.astype(F32)
     waves = wave_table(length)
     features = jnp.pad(position_features(length), ((0, 0), (0, 8 - EMB)))
-    pieces = []
+    quarters = []
     for layer_index in range(LAYERS):
         local = tuple(member[layer_index] for member in shards)
-        quarters = layer_quarters(local, mask_vector if layer_index == 0 else None)
-        pieces.append([gather_pieces(quarter, mesh_shape) for quarter in quarters])
+        quarters += layer_quarters(local, mask_vector if layer_index == 0 else None)
+    pieces = gather_all(quarters, (1, 3) * LAYERS, 1)
     hidden = hidden_in
     kept = []
     for layer_index in range(LAYERS):
         mixed = mixer_forward(
-            layer_index == 0, hidden, marked, live, waves, features, pieces[layer_index][0]
+            layer_index == 0, hidden, marked, live, waves, features, pieces[2 * layer_index]
         )
-        second = glu_forward(mixed[0], mixed[3], mixed[2], pieces[layer_index][1])
+        second = glu_forward(mixed[0], mixed[3], mixed[2], pieces[2 * layer_index + 1])
         kept.append((mixed, second))
         hidden = second[0]
     output = hidden.astype(BF16)
     grad = cotangent.astype(F32)
     layer_grads = [None] * LAYERS
-    mask_grad = None
+    totals = [None] * LAYERS
     for layer_index in reversed(range(LAYERS)):
         mixed, second = kept[layer_index]
         grad, norm_two, down_grads, glu_grads = glu_backward(
-            grad, mixed[0], mixed[3], mixed[2], second[1:], pieces[layer_index][1]
+            grad, mixed[0], mixed[3], mixed[2], second[1:], pieces[2 * layer_index + 1]
         )
-        glu = spread(scatter_sum(glu_grads, mesh_shape), mesh_shape)
         grad, mix_grads = mixer_backward(
             layer_index == 0,
             grad,
@@ -1287,11 +1502,14 @@
             norm_two,
             down_grads,
         )
-        mix = spread(scatter_sum(mix_grads, mesh_shape), mesh_shape)
+        totals[layer_index] = (mix_grads, glu_grads)
+    sums = scatter_all(totals[0] + totals[1], (1, 3) * LAYERS, 2)
+    for layer_index in reversed(range(LAYERS)):
+        mix, glu = (array.astype(F32) for array in sums[2 * layer_index : 2 * layer_index + 2])
         found, mask_grad = mix_unpack(mix.reshape(-1, mix.shape[-1]), shards)
         tall = shards[15].shape[2] // 2
-        found[15] = glu[:, :, :tall].reshape(2, 2 * tall, -1)
-        found[14] = glu[:, :, tall:].reshape(2, shards[14].shape[2], -1)
+        found[15] = glu[:, :tall].reshape(2, 2 * tall, -1)
+        found[14] = glu[:, tall:].reshape(2, shards[14].shape[2], -1)
         layer_grads[layer_index] = [found[index] for index in GRADS]
     return output, grad, mask_grad, layer_grads
 

time: 742 us -> 575 us (0.77)
  waiting for transfers between devices: 388 us -> 0 us
  Pallas kernels: 173 us -> 524 us
  starting transfers between devices: 70.9 us -> 0 us
  local copies, waits for them, and re-layouts: 50.8 us -> 20.4 us
  other arithmetic: 48.1 us -> 19.3 us
    ppermute x80 -> x0, waiting for transfers between devices: 388 us -> none  [neighbour(): return lax.ppermute(values, ('wide', 'narrow'), pairs)]
    pallas_call x0 -> x2, Pallas kernels: none -> 353 us  [the longest x1 179 us: gather_all(): pl.pallas_call(partial(gather_kernel, counts), out_shape=[jax.ShapeDtypeS...]
    ppermute x80 -> x0, starting transfers between devices: 70.9 us -> none  [neighbour(): return lax.ppermute(values, ('wide', 'narrow'), pairs)]
    convert_element_type x24 -> x0, other arithmetic: 23.3 us -> none  [the longest x20 19.8 us: total(): return (own.astype(F32) + other.astype(F32)).astype(BF16)]
    squeeze x24 -> x0, local copies, waits for them, and re-layouts: 15.3 us -> none  [the longest x4 12.1 us: scatter_sum(): both = total(parts[0], neighbour(parts[1], mesh_shape, 0, 1))]
    unnamed x150 -> x46, local copies, waits for them, and re-layouts: 15.3 us -> 7.56 us
  transfers between devices with their start and end apart: 80 -> 0, of which waited for: 40 -> 0; matrix products, arithmetic and copies ran while one was open for 9% -> 0% of each run, Pallas kernels for 14% -> 0%
where the time goes in v2:
time: 575 us; the launch traced here: 565 us
  Pallas kernels  524 us (91%)
  local copies, waits for them, and re-layouts  20.4 us (4%)
  other arithmetic  19.3 us (3%)
    pallas_call x1, Pallas kernels, gather_all(): pl.pallas_call(partial(gather_kernel, counts), out_shape=[jax.ShapeDtypeS...  179 us
    pallas_call x1, Pallas kernels, scatter_all(): pl.pallas_call(partial(scatter_kernel, counts), out_shape=[jax.ShapeDtype...  173 us
    pallas_call x8, Pallas kernels, call(): pl.pallas_call(kernel, out_shape=[jax.ShapeDtypeStruct(shape, dtype) for...  171 us

profile of v2, /device:TPU:0, one launch (start us, length us, event | category | flops | bytes accessed | tf_op | source)
XLA Modules:
  0.0 565.4 jit_solution(8804788233320292070)
XLA Ops:
  0.8 0.9 fusion
  3.4 0.7 fusion.29
  4.1 0.7 fusion.27
  4.8 0.8 fusion.26
  6.4 0.8 fusion.25
  8.6 0.8 slice_bitcast_fusion.18
  9.5 0.8 fusion.24
  10.5 0.8 copy.179
  11.3 0.8 copy.177
  12.1 0.9 slice_bitcast_fusion.22
  17.0 1.1 convert_element_type.55.grad
  18.4 0.8 pad_maximum_fusion.6.refs_3_
  19.1 0.8 pad_maximum_fusion.5.refs_1_
  19.9 179.3 %gather.1 = (bf16[2,2,2,4,80,768]{5,4,3,2,1,0:T(8,128)(2,1)}, bf16[2,2,2,4,240,768]{5,4,3,2,1,0:T(8,128)(2,1)}, bf16[2,2,2,4,80,768]{5,4,3,2,1,0:T(8,128)(2,1)}, bf16[2,2,2,4,240,768]{5,4,3,2,1,0:T(8,128)(2,1)}) custom-call(bf16[80,768]{1,0:T(8,128)(2,1)} %constant_dynamic-slice_fusion.1.refs_0_, bf16[240,768]{1,0:T(8,128)(2,1)} %pad_maximum_fusion.5.refs_1_, ...), custom_call_target="tpu_custom_call" | custom-call | tf_op jit(solution)/shard_map/gather/pallas_call | solution.py:1180
  199.2 14.5 %mixer_forward.2 = (f32[384,768]{1,0:T(8,128)}, f32[384,768]{1,0:T(8,128)}, bf16[8,320,768]{2,1,0:T(8,128)(2,1)}, f32[16,768]{1,0:T(8,128)}, f32[3,128,768]{2,1,...) custom-call(bf16[384,768]{1,0:T(8,128)(2,1)} %refs_0_.1, ...), custom_call_target="tpu_custom_call" | custom-call | flops 16999999488 | bytes 17000000 | tf_op jit(solution)/shard_map/mixer_forward/pallas_call | solution.py:941
  213.7 16.9 %glu_forward.2 = (f32[384,768]{1,0:T(8,128)}, bf16[384,768]{1,0:T(8,128)(2,1)}, bf16[2,4,384,768]{3,2,1,0:T(8,128)(2,1)}, bf16[2,4,384,768]{3,2,1,0:T(8,128)(2,1...) custom-call(f32[384,768]{1,0:T(8,128)} %get-tuple-element.77.hidden, ...), custom_call_target="tpu_custom_call" | custom-call | flops 20000000000 | bytes 20000000 | tf_op jit(solution)/shard_map/glu_forward/pallas_call | solution.py:941
  230.6 14.7 %mixer_forward.3 = (f32[384,768]{1,0:T(8,128)}, f32[384,768]{1,0:T(8,128)}, bf16[8,320,768]{2,1,0:T(8,128)(2,1)}, f32[16,768]{1,0:T(8,128)}, f32[3,128,768]{2,1,...) custom-call(f32[384,768]{1,0:T(8,128)} %get-tuple-element.81.refs_0_, ...), custom_call_target="tpu_custom_call" | custom-call | flops 16999999488 | bytes 17000000 | tf_op jit(solution)/shard_map/mixer_forward/pallas_call | solution.py:941
  245.3 16.9 %glu_forward.3 = (f32[384,768]{1,0:T(8,128)}, bf16[384,768]{1,0:T(8,128)(2,1)}, bf16[2,4,384,768]{3,2,1,0:T(8,128)(2,1)}, bf16[2,4,384,768]{3,2,1,0:T(8,128)(2,1...) custom-call(f32[384,768]{1,0:T(8,128)} %get-tuple-element.83.hidden, ...), custom_call_target="tpu_custom_call" | custom-call | flops 20000000000 | bytes 20000000 | tf_op jit(solution)/shard_map/glu_forward/pallas_call | solution.py:941
  262.2 2.1 convert_element_type.54
  264.3 32.7 %glu_backward.2 = (f32[384,768]{1,0:T(8,128)}, f32[8,768]{1,0:T(8,128)}, bf16[6,4,192,192]{3,2,1,0:T(8,128)(2,1)}, bf16[2,2,2,4,240,768]{5,4,3,2,1,0:T(8,128)(2,1)}) custom-call(f32[384,768]{1,0:T(8,128)} %convert_element_type.55.grad, f32[384,768]{1,0:T(8,128)} %get-tuple-element.83.hidden, f32[16,768]{1,0:T(8,128)} %get-tuple-element.84.table.refs_7_, ...), custom_call_target="tpu_custom_call" | custom-call | flops 38000001024 | bytes 38000000 | tf_op jit(solution)/shard_map/glu_backward/pallas_call | solution.py:941
  297.1 21.3 %mixer_backward.2 = (f32[384,768]{1,0:T(8,128)}, bf16[2,2,2,4,80,768]{5,4,3,2,1,0:T(8,128)(2,1)}) custom-call(f32[384,768]{1,0:T(8,128)} %get-tuple-element.93.refs_0_, f32[384,768]{1,0:T(8,128)} %get-tuple-element.94.refs_1_, f32[384,1]{1,0:T(8,128)} %bitcast.171, f32[384,1]{1,0:T(8,128)} %bitcast.167, bf16[2,256,128]{2,1,0:T(8,128)(2,1)} %constant.180.refs_3_.refs_4_, ...), custom_call_target="tpu_custom_call" | custom-call | flops 24000000000 | bytes 24000000 | tf_op jit(solution)/shard_map/mixer_backward/pallas_call | solution.py:941
  318.4 32.7 %glu_backward.3 = (f32[384,768]{1,0:T(8,128)}, f32[8,768]{1,0:T(8,128)}, bf16[6,4,192,192]{3,2,1,0:T(8,128)(2,1)}, bf16[2,2,2,4,240,768]{5,4,3,2,1,0:T(8,128)(2,1)}) custom-call(f32[384,768]{1,0:T(8,128)} %get-tuple-element.105.grad, f32[384,768]{1,0:T(8,128)} %get-tuple-element.77.hidden, f32[16,768]{1,0:T(8,128)} %get-tuple-element.78.table.refs_7_, ...), custom_call_target="tpu_custom_call" | custom-call | flops 38000001024 | bytes 38000000 | tf_op jit(solution)/shard_map/glu_backward/pallas_call | solution.py:941
  351.1 21.5 %mixer_backward.3 = (f32[384,768]{1,0:T(8,128)}, bf16[2,2,2,4,80,768]{5,4,3,2,1,0:T(8,128)(2,1)}) custom-call(f32[384,768]{1,0:T(8,128)} %get-tuple-element.111.refs_0_, f32[384,768]{1,0:T(8,128)} %get-tuple-element.112.refs_1_, f32[384,1]{1,0:T(8,128)} %bitcast.172, f32[384,1]{1,0:T(8,128)} %bitcast.168, bf16[2,256,128]{2,1,0:T(8,128)(2,1)} %constant.180.refs_3_.refs_4_, ...), custom_call_target="tpu_custom_call" | custom-call | flops 24000000000 | bytes 24000000 | tf_op jit(solution)/shard_map/mixer_backward/pallas_call | solution.py:941
  372.6 173.5 %scatter.1 = (bf16[4,80,768]{2,1,0:T(8,128)(2,1)}, bf16[4,240,768]{2,1,0:T(8,128)(2,1)}, bf16[4,80,768]{2,1,0:T(8,128)(2,1)}, bf16[4,240,768]{2,1,0:T(8,128)(2,1)}) custom-call(bf16[2,2,2,4,80,768]{5,4,3,2,1,0:T(8,128)(2,1)} %get-tuple-element.124.refs_0_, bf16[2,2,2,4,240,768]{5,4,3,2,1,0:T(8,128)(2,1)} %get-tuple-element.125.refs_1_, ...), custom_call_target="tpu_custom_call" | custom-call | tf_op jit(solution)/shard_map/scatter/pallas_call | solution.py:1309
  546.1 1.1 bitcast_convert_fusion.1
  548.3 1.1 copy-done
  550.0 1.1 pad_maximum_fusion.1
  551.5 2.5 pad_maximum_fusion
  559.1 0.8 copy.156
  562.2 0.8 pad_maximum_fusion.4
  563.0 0.8 pad_maximum_fusion.3
  563.9 1.1 copy.157
  (124 shorter events, 17.6 us)
Async XLA Ops:
  0.7 12.5 %copy-start.3 = (bf16[2,128,192]{1,2,0:T(8,128)(2,1)S(1)}, bf16[2,128,192]{1,2,0:T(8,128)(2,1)}, u32[]{:S(2)}) copy-start(bf16[2,128,192]{1,2,0:T(8,128)(2,1)} %param.39) | copy-start | bytes 294916
  0.7 12.4 %copy-start.9 = (bf16[2,96,192]{2,1,0:T(8,128)(2,1)S(1)}, bf16[2,96,192]{2,1,0:T(8,128)(2,1)}, u32[]{:S(2)}) copy-start(bf16[2,96,192]{2,1,0:T(8,128)(2,1)} %param.46) | copy-start | bytes 221188
  0.7 13.1 %copy-start.6 = (bf16[2,384,192]{1,2,0:T(8,128)(2,1)S(1)}, bf16[2,384,192]{1,2,0:T(8,128)(2,1)}, u32[]{:S(2)}) copy-start(bf16[2,384,192]{1,2,0:T(8,128)(2,1)} %param.45) | copy-start | bytes 884740
  0.7 12.4 %copy-start.10 = (bf16[2,96,192]{2,1,0:T(8,128)(2,1)S(1)}, bf16[2,96,192]{2,1,0:T(8,128)(2,1)}, u32[]{:S(2)}) copy-start(bf16[2,96,192]{2,1,0:T(8,128)(2,1)} %param.42) | copy-start | bytes 221188
  0.7 12.3 %copy-start.8 = (bf16[2,2,96,192]{3,2,1,0:T(8,128)(2,1)S(1)}, bf16[2,2,96,192]{3,2,1,0:T(8,128)(2,1)}, u32[]{:S(2)}) copy-start(bf16[2,2,96,192]{3,2,1,0:T(8,128)(2,1)} %param.32) | copy-start | bytes 442372
  13.9 2.9 copy-start.5
  14.9 2.0 copy-start.4
  16.2 1.9 copy-start.2
  548.0 1.4 copy-start
  548.3 1.7 copy-start.1
  551.5 2.5 copy-start.7

commit v3 on v2

--- a/solution.py
+++ b/solution.py
@@ -952,12 +952,9 @@
     )(*operands)
 
 
-def mixer_forward(first_layer, hidden, marked, live, waves, features, pieces):
-    rows, width = hidden.shape
-    length = waves.shape[2]
+def mixer_outs(rows, width, length, quarter):
     block = width // BLOCKS
-    quarter = pieces.shape[4]
-    outs = [
+    return [
         ((rows, width), F32),
         ((rows, width), F32),
         ((8, 4 * quarter, width), BF16),
@@ -971,29 +968,23 @@
         ((rows, width), BF16),
         ((BLOCKS, rows, block), BF16),
     ]
-    operands = (hidden, marked, live, waves, features, pieces)
-    return call(
-        partial(mixer_forward_kernel, first_layer),
-        "mixer_forward",
-        outs,
-        operands,
-        (5,),
-        (),
-        [pltpu.SemaphoreType.DMA((32,))],
-    )
-
-
-def glu_forward(hidden, table, mix, pieces):
-    rows, width = hidden.shape
-    block = width // BLOCKS
-    outs = [
+
+
+def glu_outs(rows, width):
+    return [
         ((rows, width), F32),
         ((rows, width), BF16),
         ((2, BLOCKS, rows, width), BF16),
         ((2, BLOCKS, rows, width), BF16),
         ((BLOCKS, rows, width), BF16),
-        ((BLOCKS, rows, block), BF16),
+        ((BLOCKS, rows, width // BLOCKS), BF16),
     ]
+
+
+def glu_forward(hidden, table, mix, pieces):
+    rows, width = hidden.shape
+    block = width // BLOCKS
+    outs = glu_outs(rows, width)
     return call(
         glu_forward_kernel,
         "glu_forward",
@@ -1137,30 +1128,54 @@
     yield
 
 
-def pipeline(starts, ahead):
+def pipeline(starts, between):
     running = []
     waiting = list(starts)
+    number = 0
     while waiting or running:
         if waiting:
             running.append(waiting.pop(0)())
-        for chunk in list(running):
+        for chunk in reversed(list(running)):
             try:
                 next(chunk)
             except StopIteration:
                 running.remove(chunk)
-
-
-def gather_kernel(counts, *refs):
+        if number in between:
+            between[number]()
+        number += 1
+
+
+def save_all(sources, targets, sems, first):
+    copies = [
+        pltpu.make_async_copy(source, target, sems.at[first + index])
+        for index, (source, target) in enumerate(zip(sources, targets))
+    ]
+    start_all(copies)
+    return copies
+
+
+MIXER_OUTS, GLU_OUTS = 12, 6
+
+
+def forward_kernel(counts, *refs):
     groups = len(counts)
-    owns, pieces = refs[:groups], refs[groups : 2 * groups]
-    sent, received, local = refs[2 * groups :]
+    owns, refs = refs[:groups], refs[groups:]
+    hidden_in, marked, live, waves, features = refs[:5]
+    pieces, refs = refs[5 : 5 + groups], refs[5 + groups :]
+    first_outs, refs = refs[:MIXER_OUTS], refs[MIXER_OUTS:]
+    glu_outs, refs = refs[:GLU_OUTS], refs[GLU_OUTS:]
+    second_outs, refs = refs[:MIXER_OUTS], refs[MIXER_OUTS:]
+    mixer, refs = refs[:MIXER_OUTS], refs[MIXER_OUTS:]
+    glu, refs = refs[:GLU_OUTS], refs[GLU_OUTS:]
+    staged, refs = refs[:groups], refs[groups:]
+    left, right, parts, sent, received, local, loads = refs
     mail = Mail(sent, received)
+    copies = [
+        pltpu.make_async_copy(own, stage, local.at[index])
+        for index, (own, stage) in enumerate(zip(owns, staged))
+    ]
+    start_all(copies)
     greet()
-    copies = []
-    for index in range(groups):
-        copy = pltpu.make_async_copy(owns[index], pieces[index].at[0, 0, 0, 0], local.at[index])
-        copy.start()
-        copies.append(copy)
     starts = []
     for index, count in enumerate(counts):
         size = owns[index].shape[0] // count
@@ -1170,29 +1185,79 @@
                 partial(gather_steps, mail, owns[index].at[rows], pieces[index], rows)
             )
     wait_all(copies)
-    pipeline(starts, 1)
+    own_copies = save_all(
+        staged, [array.at[0, 0, 0, 0] for array in pieces], local, groups
+    )
+    saves = []
+
+    def store_own():
+        wait_all(own_copies)
+
+    def first_mixer():
+        mixer_forward_kernel(
+            True, hidden_in, marked, live, waves, features, pieces[0], *mixer, loads
+        )
+        saves.extend(save_all(mixer, first_outs, local, 2 * groups))
+
+    def first_glu():
+        glu_forward_kernel(
+            mixer[0], mixer[3], mixer[2], pieces[1], *glu, left, right, parts, loads
+        )
+        saves.extend(save_all(glu, glu_outs, local, 2 * groups + MIXER_OUTS))
+
+    def second_mixer():
+        wait_all(saves[:MIXER_OUTS])
+        mixer_forward_kernel(
+            False, glu[0], marked, live, waves, features, pieces[2], *mixer, loads
+        )
+        saves.extend(save_all(mixer, second_outs, local, 2 * groups + MIXER_OUTS + GLU_OUTS))
+
+    ready = [sum(counts[: index + 1]) + 3 for index in range(3)]
+    pipeline(
+        starts, {0: store_own, ready[0]: first_mixer, ready[1]: first_glu, ready[2]: second_mixer}
+    )
+    wait_all(saves[MIXER_OUTS:])
     mail.finish()
 
 
-def gather_all(quarters, counts, number):
+def forward(quarters, counts, hidden, marked, live, waves, features, number):
+    rows, width = hidden.shape
+    groups = len(counts)
     anywhere = pl.BlockSpec(memory_space=pl.ANY)
+    vmem = pl.BlockSpec(memory_space=pltpu.VMEM)
     total = GATHER_COPIES * sum(counts)
-    return pl.pallas_call(
-        partial(gather_kernel, counts),
-        out_shape=[
-            jax.ShapeDtypeStruct((2, 2, 2, 4) + quarter.shape, quarter.dtype)
-            for quarter in quarters
-        ],
-        in_specs=[anywhere] * len(quarters),
-        out_specs=[anywhere] * len(quarters),
-        scratch_shapes=[
+    mixer = mixer_outs(rows, width, waves.shape[2], quarters[0].shape[0])
+    glu = glu_outs(rows, width)
+    outs = [((2, 2, 2, 4) + quarter.shape, BF16) for quarter in quarters] + mixer + glu + mixer
+    block = width // BLOCKS
+    result = pl.pallas_call(
+        partial(forward_kernel, counts),
+        out_shape=[jax.ShapeDtypeStruct(shape, dtype) for shape, dtype in outs],
+        in_specs=[anywhere] * groups + [vmem] * 5,
+        out_specs=[anywhere] * len(outs),
+        scratch_shapes=[pltpu.VMEM(shape, dtype) for shape, dtype in mixer + glu]
+        + [pltpu.VMEM(quarter.shape, BF16) for quarter in quarters]
+        + [
+            pltpu.VMEM((2, BLOCKS, width, width), BF16),
+            pltpu.VMEM((2, width, width), BF16),
+            pltpu.VMEM((BLOCKS, rows, block), F32),
             pltpu.SemaphoreType.DMA((total,)),
             pltpu.SemaphoreType.DMA((total,)),
-            pltpu.SemaphoreType.DMA((len(quarters),)),
+            pltpu.SemaphoreType.DMA((2 * groups + 2 * MIXER_OUTS + GLU_OUTS,)),
+            pltpu.SemaphoreType.DMA((64,)),
         ],
-        compiler_params=pltpu.CompilerParams(collective_id=number, has_side_effects=True),
-        name="gather",
-    )(*quarters)
+        compiler_params=pltpu.CompilerParams(
+            collective_id=number, has_side_effects=True, vmem_limit_bytes=VMEM_BYTES
+        ),
+        name="forward",
+    )(*quarters, hidden, marked, live, waves, features)
+    pieces, result = result[:groups], result[groups:]
+    return (
+        pieces,
+        result[:MIXER_OUTS],
+        result[MIXER_OUTS : MIXER_OUTS + GLU_OUTS],
+        result[MIXER_OUTS + GLU_OUTS :],
+    )
 
 
 SCATTER_COPIES = 11
@@ -1293,7 +1358,7 @@
                     buffers[8 * number : 8 * number + 8],
                 )
             )
-    pipeline(starts, 1)
+    pipeline(starts, {})
     mail.finish()
 
 
@@ -1472,16 +1537,14 @@
     for layer_index in range(LAYERS):
         local = tuple(member[layer_index] for member in shards)
         quarters += layer_quarters(local, mask_vector if layer_index == 0 else None)
-    pieces = gather_all(quarters, (1, 3) * LAYERS, 1)
-    hidden = hidden_in
-    kept = []
-    for layer_index in range(LAYERS):
-        mixed = mixer_forward(
-            layer_index == 0, hidden, marked, live, waves, features, pieces[2 * layer_index]
-        )
-        second = glu_forward(mixed[0], mixed[3], mixed[2], pieces[2 * layer_index + 1])
-        kept.append((mixed, second))
-        hidden = second[0]
+    pieces, mixed, second, mixed_two = forward(
+        quarters, (1, 3) * LAYERS, hidden_in, marked, live, waves, features, 1
+    )
+    kept = [
+        (mixed, second),
+        (mixed_two, glu_forward(mixed_two[0], mixed_two[3], mixed_two[2], pieces[3])),
+    ]
+    hidden = kept[1][1][0]
     output = hidden.astype(BF16)
     grad = cotangent.astype(F32)
     layer_grads = [None] * LAYERS

time: 575 us -> 500 us (0.87)
  Pallas kernels: 524 us -> 450 us
    pallas_call x8 -> x5, Pallas kernels: 171 us -> 125 us  [call(): pl.pallas_call(kernel, out_shape=[jax.ShapeDtypeStruct(shape, dtype) for...]
    pallas_call x1, Pallas kernels: 179 us -> 149 us  [forward(): pl.pallas_call(partial(forward_kernel, counts), out_shape=[jax.ShapeDtype...]
where the time goes in v3:
time: 500 us; the launch traced here: 491 us
  Pallas kernels  450 us (90%)
  local copies, waits for them, and re-layouts  20.4 us (4%)
  other arithmetic  19.3 us (4%)
    pallas_call x1, Pallas kernels, scatter_all(): pl.pallas_call(partial(scatter_kernel, counts), out_shape=[jax.ShapeDtype...  175 us
    pallas_call x1, Pallas kernels, forward(): pl.pallas_call(partial(forward_kernel, counts), out_shape=[jax.ShapeDtype...  149 us
    pallas_call x5, Pallas kernels, call(): pl.pallas_call(kernel, out_shape=[jax.ShapeDtypeStruct(shape, dtype) for...  125 us
    another operation x23, other arithmetic, body(): jnp.stack([layer_grads[position][member_index] for position in range(LAYE...  10.9 us

profile of v3, /device:TPU:0, one launch (start us, length us, event | category | flops | bytes accessed | tf_op | source)
XLA Modules:
  0.0 491.0 jit_solution(14126967271873590117)
XLA Ops:
  0.8 0.9 fusion
  1.9 0.7 convert_bitcast_fusion
  3.4 0.7 fusion.29
  4.1 0.7 fusion.27
  4.8 0.8 fusion.26
  5.7 0.7 concatenate.62
  6.4 0.8 fusion.25
  7.2 0.7 slice_bitcast_fusion.34
  8.6 0.8 slice_bitcast_fusion.18
  9.4 0.8 fusion.24
  10.5 0.8 copy.173
  11.3 0.8 copy.171
  12.1 0.9 slice_bitcast_fusion.22
  17.0 1.1 convert_element_type.55.grad
  18.4 0.8 pad_maximum_fusion.6.refs_3_
  19.1 0.8 pad_maximum_fusion.5.refs_1_
  19.9 149.0 %forward.1 = (bf16[2,2,2,4,80,768]{5,4,3,2,1,0:T(8,128)(2,1)}, bf16[2,2,2,4,240,768]{5,4,3,2,1,0:T(8,128)(2,1)}, bf16[2,2,2,4,80,768]{5,4,3,2,1,0:T(8,128)(2,1)}...) custom-call(bf16[80,768]{1,0:T(8,128)(2,1)} %constant_dynamic-slice_, ...), custom_call_target="tpu_custom_call" | custom-call | tf_op jit(solution)/shard_map/forward/pallas_call | solution.py:1233
  168.9 16.9 %glu_forward.1 = (f32[384,768]{1,0:T(8,128)}, bf16[384,768]{1,0:T(8,128)(2,1)}, bf16[2,4,384,768]{3,2,1,0:T(8,128)(2,1)}, bf16[2,4,384,768]{3,2,1,0:T(8,128)(2,1...) custom-call(f32[384,768]{1,0:T(8,128)} %get-tuple-element.73.hidden, ...), custom_call_target="tpu_custom_call" | custom-call | flops 20000000000 | bytes 20000000 | tf_op jit(solution)/shard_map/glu_forward/pallas_call | solution.py:941
  185.8 2.1 convert_element_type.54
  187.9 32.7 %glu_backward.2 = (f32[384,768]{1,0:T(8,128)}, f32[8,768]{1,0:T(8,128)}, bf16[6,4,192,192]{3,2,1,0:T(8,128)(2,1)}, bf16[2,2,2,4,240,768]{5,4,3,2,1,0:T(8,128)(2,1)}) custom-call(f32[384,768]{1,0:T(8,128)} %convert_element_type.55.grad, f32[384,768]{1,0:T(8,128)} %get-tuple-element.73.hidden, f32[16,768]{1,0:T(8,128)} %get-tuple-element.74.table.refs_7_, ...), custom_call_target="tpu_custom_call" | custom-call | flops 38000001024 | bytes 38000000 | tf_op jit(solution)/shard_map/glu_backward/pallas_call | solution.py:941
  220.6 21.3 %mixer_backward.2 = (f32[384,768]{1,0:T(8,128)}, bf16[2,2,2,4,80,768]{5,4,3,2,1,0:T(8,128)(2,1)}) custom-call(f32[384,768]{1,0:T(8,128)} %get-tuple-element.83.refs_0_, f32[384,768]{1,0:T(8,128)} %get-tuple-element.84.refs_1_, f32[384,1]{1,0:T(8,128)} %bitcast.169, f32[384,1]{1,0:T(8,128)} %bitcast.166, bf16[2,256,128]{2,1,0:T(8,128)(2,1)} %constant.180.refs_7_.refs_4_, ...), custom_call_target="tpu_custom_call" | custom-call | flops 24000000000 | bytes 24000000 | tf_op jit(solution)/shard_map/mixer_backward/pallas_call | solution.py:941
  241.9 32.8 %glu_backward.3 = (f32[384,768]{1,0:T(8,128)}, f32[8,768]{1,0:T(8,128)}, bf16[6,4,192,192]{3,2,1,0:T(8,128)(2,1)}, bf16[2,2,2,4,240,768]{5,4,3,2,1,0:T(8,128)(2,1)}) custom-call(f32[384,768]{1,0:T(8,128)} %get-tuple-element.95.grad, f32[384,768]{1,0:T(8,128)} %get-tuple-element.96.hidden, f32[16,768]{1,0:T(8,128)} %get-tuple-element.97.table.refs_7_, ...), custom_call_target="tpu_custom_call" | custom-call | flops 38000001024 | bytes 38000000 | tf_op jit(solution)/shard_map/glu_backward/pallas_call | solution.py:941
  274.7 21.5 %mixer_backward.3 = (f32[384,768]{1,0:T(8,128)}, bf16[2,2,2,4,80,768]{5,4,3,2,1,0:T(8,128)(2,1)}) custom-call(f32[384,768]{1,0:T(8,128)} %get-tuple-element.105.refs_0_, f32[384,768]{1,0:T(8,128)} %get-tuple-element.106.refs_1_, f32[384,1]{1,0:T(8,128)} %bitcast.170, f32[384,1]{1,0:T(8,128)} %bitcast.167, bf16[2,256,128]{2,1,0:T(8,128)(2,1)} %constant.180.refs_7_.refs_4_, ...), custom_call_target="tpu_custom_call" | custom-call | flops 24000000000 | bytes 24000000 | tf_op jit(solution)/shard_map/mixer_backward/pallas_call | solution.py:941
  296.3 175.4 %scatter.1 = (bf16[4,80,768]{2,1,0:T(8,128)(2,1)}, bf16[4,240,768]{2,1,0:T(8,128)(2,1)}, bf16[4,80,768]{2,1,0:T(8,128)(2,1)}, bf16[4,240,768]{2,1,0:T(8,128)(2,1)}) custom-call(bf16[2,2,2,4,80,768]{5,4,3,2,1,0:T(8,128)(2,1)} %get-tuple-element.118.refs_0_, bf16[2,2,2,4,240,768]{5,4,3,2,1,0:T(8,128)(2,1)} %get-tuple-element.119.refs_1_, ...), custom_call_target="tpu_custom_call" | custom-call | tf_op jit(solution)/shard_map/scatter/pallas_call | solution.py:1374
  471.7 1.1 bitcast_convert_fusion.1
  473.9 1.1 copy-done
  475.5 1.1 pad_maximum_fusion.1
  477.1 2.5 pad_maximum_fusion
  484.7 0.8 copy.150
  487.8 0.8 pad_maximum_fusion.4
  488.6 0.8 pad_maximum_fusion.3
  489.5 1.1 copy.151
  (121 shorter events, 15.4 us)
Async XLA Ops:
  0.7 12.4 %copy-start.3 = (bf16[2,128,192]{1,2,0:T(8,128)(2,1)S(1)}, bf16[2,128,192]{1,2,0:T(8,128)(2,1)}, u32[]{:S(2)}) copy-start(bf16[2,128,192]{1,2,0:T(8,128)(2,1)} %param.39) | copy-start | bytes 294916
  0.7 12.4 %copy-start.9 = (bf16[2,96,192]{2,1,0:T(8,128)(2,1)S(1)}, bf16[2,96,192]{2,1,0:T(8,128)(2,1)}, u32[]{:S(2)}) copy-start(bf16[2,96,192]{2,1,0:T(8,128)(2,1)} %param.46) | copy-start | bytes 221188
  0.7 13.1 %copy-start.6 = (bf16[2,384,192]{1,2,0:T(8,128)(2,1)S(1)}, bf16[2,384,192]{1,2,0:T(8,128)(2,1)}, u32[]{:S(2)}) copy-start(bf16[2,384,192]{1,2,0:T(8,128)(2,1)} %param.45) | copy-start | bytes 884740
  0.7 12.4 %copy-start.10 = (bf16[2,96,192]{2,1,0:T(8,128)(2,1)S(1)}, bf16[2,96,192]{2,1,0:T(8,128)(2,1)}, u32[]{:S(2)}) copy-start(bf16[2,96,192]{2,1,0:T(8,128)(2,1)} %param.42) | copy-start | bytes 221188
  0.7 12.3 %copy-start.8 = (bf16[2,2,96,192]{3,2,1,0:T(8,128)(2,1)S(1)}, bf16[2,2,96,192]{3,2,1,0:T(8,128)(2,1)}, u32[]{:S(2)}) copy-start(bf16[2,2,96,192]{3,2,1,0:T(8,128)(2,1)} %param.32) | copy-start | bytes 442372
  13.9 2.9 copy-start.5
  14.9 2.0 copy-start.4
  16.2 1.9 copy-start.2
  473.6 1.4 copy-start
  473.8 1.7 copy-start.1
  477.0 2.5 copy-start.7
